TPU v7x, 128 devices: a whole 4x4x4 slice. The times are simulated.
128 devices in a mesh: fsdp: 128 (over x, z, y, core).
Axes of the slice: x: 4, y: 4, z: 4, core: 2. Of those that a mesh axis runs over, the one named last changes fastest.
Arguments:
- tokens: bfloat16 [2, 16384, 1024], P(None, 'fsdp'), may hold values from -6 to 6
- cotangent: bfloat16 [2, 16384, 1024], P(None, 'fsdp'), may hold values from -6 to 6
- decays: bfloat16 [2, 16384, 24], P(None, 'fsdp'), as said below
- route: int32 [2, 16384], replicated, may hold values from 0 to 16383, as said below
- lengths: int32 [2, 128, 2], P(None, 'fsdp'), may hold values from 0 to 128, as said below
- adapter_ids: int32 [2, 128, 2], P(None, 'fsdp'), may hold values from 0 to 7
- gain_mix: float32 [1024], replicated, may hold values from 0.5 to 1.5
- gain_ffn: float32 [1024], replicated, may hold values from 0.5 to 1.5
- persistent: bfloat16 [2, 16, 1024], replicated, may hold values from -6 to 6
- w_in: bfloat16 [1024, 7168], P('fsdp'), may hold values from -0.1875 to 0.1875
- w_out: bfloat16 [1024, 1024], P('fsdp'), may hold values from -0.5 to 0.5
- w_up: bfloat16 [1024, 5632], P('fsdp'), may hold values from -0.1875 to 0.1875
- w_down: bfloat16 [2816, 1024], P('fsdp'), may hold values from -0.109375 to 0.109375
- in_down: bfloat16 [8, 1024, 112], P(None, 'fsdp'), may hold values from -0.1875 to 0.1875
- in_up: bfloat16 [8, 112, 1024], P(None, None, 'fsdp'), may hold values from -1.5 to 1.5
- out_down: bfloat16 [8, 1024, 16], P(None, 'fsdp'), may hold values from -0.1875 to 0.1875
- out_up: bfloat16 [8, 16, 1024], P(None, None, 'fsdp'), may hold values from -1.5 to 1.5
- up_down: bfloat16 [8, 1024, 32], P(None, 'fsdp'), may hold values from -0.1875 to 0.1875
- up_up: bfloat16 [8, 32, 2816], P(None, None, 'fsdp'), may hold values from -1.5 to 1.5
- down_down: bfloat16 [8, 2816, 16], P(None, 'fsdp'), may hold values from -0.109375 to 0.109375
- down_up: bfloat16 [8, 16, 1024], P(None, None, 'fsdp'), may hold values from -1.5 to 1.5
Outputs:
- activations: bfloat16 [2, 16384, 1024], P(None, 'fsdp')
- input_grad: bfloat16 [2, 16384, 1024], P(None, 'fsdp')
- grad_in_down: float32 [8, 1024, 112], P(None, 'fsdp')
- grad_in_up: float32 [8, 112, 1024], P(None, None, 'fsdp')
- grad_out_down: float32 [8, 1024, 16], P(None, 'fsdp')
- grad_out_up: float32 [8, 16, 1024], P(None, None, 'fsdp')
- grad_up_down: float32 [8, 1024, 32], P(None, 'fsdp')
- grad_up_up: float32 [8, 32, 2816], P(None, None, 'fsdp')
- grad_down_down: float32 [8, 2816, 16], P(None, 'fsdp')
- grad_down_up: float32 [8, 16, 1024], P(None, None, 'fsdp')
Inputs may be any that keep to these rules, and one draw needn't show every extreme that they name: route[m] is a permutation; of the 128 tokens in each aligned block of route's second dimension, exactly one goes to each aligned block of 128 working rows. Each group's lengths are multiples of 64 that sum to 128; zeros only after the last sequence. `decays`: retention and momentum lie in (0, 1], steps are positive.
All inputs are finite; a program needn't handle non-finite values.
Results may differ from a plain program's by a relative error of at most 0.018.
The roundings to bfloat16 on the way count: a program that leaves them out, or rounds other values in their place, can miss the bound.
Values may be sent and summed in bfloat16 or wider, within the bound.
A program may use at most 256 MiB of HBM per device.

v0:
```python
import functools
import math

import jax
import jax.numpy as jnp
from jax import lax
from jax.experimental import pallas as pl
from jax.experimental.pallas import tpu as pltpu
from jax.sharding import PartitionSpec as P

D = 1024
H = 8
HEAD = 128
FF = 2816
R = 16
NAD = 8
NP = 16
SPAN = 64
GROUP = 128
MB = 2
ROWS = MB * GROUP
N_DEV = 128
AR = NAD * R
HCOLS = 7 * HEAD
FF_SHARD = FF // N_DEV
FF_PAD = 24
FFP = FF_PAD * N_DEV
FB = 1024
EPS = 1e-05
SCALE = 1.0 / math.sqrt(HEAD)
VMEM_LIMIT = 60 * 1024 * 1024
BF = jnp.bfloat16
F32 = jnp.float32

NN = (((1,), (0,)), ((), ()))
NT = (((1,), (1,)), ((), ()))
TN = (((0,), (0,)), ((), ()))


def dot(left, right, dims=NN):
    return lax.dot_general(left, right, dims, preferred_element_type=F32)


def exact(left, right, dims=NN):
    return lax.dot_general(
        left, right, dims, precision=lax.Precision.HIGHEST, preferred_element_type=F32
    )


def halves(value):
    high = value.astype(BF)
    return high, (value - high.astype(F32)).astype(BF)


def dot3(left, right, dims=NN):
    lh, ll = left
    rh, rl = right
    return dot(lh, rh, dims) + (dot(lh, rl, dims) + dot(ll, rh, dims))


def norm_fwd(values, gain):
    inv = lax.rsqrt(jnp.mean(values * values, axis=-1, keepdims=True) + EPS)
    return values * inv * gain, inv


def norm_bwd(grad, values, inv, gain):
    scaled = grad * gain
    return inv * (scaled - values * (inv * inv * jnp.mean(values * scaled, axis=-1, keepdims=True)))


def decay_kernel(split_ref, dec_ref, dect_ref, wf_ref, lw_ref):
    rows = lax.broadcasted_iota(jnp.int32, (GROUP, GROUP), 0)
    cols = lax.broadcasted_iota(jnp.int32, (GROUP, GROUP), 1)
    lower = (rows >= cols) & ((rows >= SPAN) == (cols >= SPAN))
    tri = lower.astype(F32)
    second = rows >= SPAN
    for g in range(MB):
        keep = 1.0 - split_ref[g]
        here = dec_ref[g * GROUP : (g + 1) * GROUP, :]
        here_t = dect_ref[:, g * GROUP : (g + 1) * GROUP]
        run = exact(tri, jnp.log(here[:, : 2 * H]))
        run_t = exact(jnp.log(here_t[: 2 * H, :]), tri, NT)
        for h in range(H):
            gap = run[:, h : h + 1] - run_t[h : h + 1, :]
            retain = jnp.exp(jnp.where(lower, gap, -1e30))
            gap = run[:, H + h : H + h + 1] - run_t[H + h : H + h + 1, :]
            moment = jnp.exp(jnp.where(lower, gap, -1e30))
            pairs = exact(retain, moment)
            theta = here_t[2 * H + h : 2 * H + h + 1, :]
            moment_run = jnp.exp(run_t[H + h : H + h + 1, :])
            carry = jnp.sum(retain * moment_run, axis=1, keepdims=True)
            last_weight = pairs[SPAN - 1 : SPAN, :] * theta * keep
            last_moment = moment[SPAN - 1 : SPAN, :] * theta * keep
            across = jnp.exp(run[:, h : h + 1]) * last_weight + carry * last_moment
            wf_ref[h, g] = pairs * theta + jnp.where(second, across, 0.0)
            lw_ref[h, g] = jnp.broadcast_to(last_weight, (8, GROUP))


def allowed_mask(split_ref):
    rows = lax.broadcasted_iota(jnp.int32, (ROWS, GROUP), 0)
    cols = lax.broadcasted_iota(jnp.int32, (ROWS, GROUP), 1)
    local = rows % GROUP
    group = rows // GROUP
    split = jnp.where(group == 0, split_ref[0], split_ref[1]) > 0.5
    return (local >= cols) & jnp.logical_not(split & (local >= SPAN) & (cols < SPAN))


def by_group(make):
    return jnp.concatenate([make(slice(0, GROUP), 0), make(slice(GROUP, ROWS), 1)], axis=0)


def attend(q, k, v, pk, pv, allowed):
    near = by_group(lambda s, g: dot(q[s], k[s], NT))
    far = dot(q, pk, NT) * SCALE
    near = jnp.where(allowed, near * SCALE, -1000000000.0)
    top = jnp.maximum(
        jnp.max(near, axis=-1, keepdims=True), jnp.max(far, axis=-1, keepdims=True)
    )
    near = jnp.exp(near - top)
    far = jnp.exp(far - top)
    inv = 1.0 / (jnp.sum(near, axis=-1, keepdims=True) + jnp.sum(far, axis=-1, keepdims=True))
    near = near * inv
    far = far * inv
    return near, far


def attend_out(near_half, far_half, v, pv):
    return by_group(lambda s, g: dot(near_half[s], v[s])) + dot(far_half, pv)


def unit(values):
    inv = lax.rsqrt(jnp.mean(values * values, axis=-1, keepdims=True) + EPS)
    return values * (inv * SCALE), inv


def unit_bwd(grad, values, inv):
    return (inv * SCALE) * (
        grad - values * (inv * inv * jnp.mean(values * grad, axis=-1, keepdims=True))
    )


def plain(value):
    return (value.astype(BF),)


def dot1(left, right, dims=NN):
    return dot(left[0], right[0], dims)


def memory_terms(kn, qn, mv, wf_ref, lw_ref, halves=halves, dot3=dot3):
    second = lax.broadcasted_iota(jnp.int32, (GROUP, GROUP), 0) >= SPAN
    kept = []
    for g in range(MB):
        s = slice(g * GROUP, (g + 1) * GROUP)
        kh, qh = halves(kn[s]), halves(qn[s])
        wf = wf_ref[0, g]
        lw = jnp.where(second, lw_ref[0, g][0:1, :], 0.0)
        kk = dot3(kh, kh, NT) * lw
        qk = dot3(qh, kh, NT) * wf
        kk_half = halves(kk)
        mvh = halves(mv[s])
        err = mv[s] - dot3(kk_half, mvh)
        errh = halves(err)
        qk_half = halves(qk)
        kept.append((kh, qh, wf, lw, kk_half, qk_half, mvh, errh))
    return kept


def memory_out(kept, dot3=dot3):
    return jnp.concatenate([dot3(item[5], item[7]) for item in kept], axis=0)


def memory_bwd(kept, grad, halves=plain, dot3=dot1):
    grads_k, grads_q, grads_v = [], [], []
    for g in range(MB):
        kh, qh, wf, lw, kk_half, qk_half, mvh, errh = kept[g]
        gh = halves(grad[g * GROUP : (g + 1) * GROUP])
        d_qk = dot3(gh, errh, NT) * wf
        d_err = dot3(qk_half, gh, TN)
        deh = halves(d_err)
        d_v = d_err - dot3(kk_half, deh, TN)
        d_kk = dot3(deh, mvh, NT) * lw
        dqh = halves(d_qk)
        dkh = halves(d_kk)
        grads_q.append(dot3(dqh, kh))
        grads_k.append(dot3(dqh, qh, TN) - (dot3(dkh, kh) + dot3(dkh, kh, TN)))
        grads_v.append(d_v)
    return (
        jnp.concatenate(grads_k, axis=0),
        jnp.concatenate(grads_q, axis=0),
        jnp.concatenate(grads_v, axis=0),
    )


AXES = ("x", "z", "y")
MESH = pl.DeviceIdType.MESH


def position():
    me = lax.axis_index("fsdp")
    chip = me // 2
    return me % 2, (chip // 16, (chip // 4) % 4, chip % 4)


def device(core, spot):
    return (((spot[0] * 4 + spot[1]) * 4 + spot[2]) * 2 + core,)


def moved(spot, axis, by):
    return tuple((v + by + 4) % 4 if i == axis else v for i, v in enumerate(spot))


def cut(lanes, count):
    base, extra = divmod(lanes, count)
    runs, at = [], 0
    for i in range(count):
        size = base + (1 if i < extra else 0)
        runs.append((at * 128, size * 128))
        at += size
    return runs


def neighbours(core, spot):
    found = {}
    for axis in range(3):
        for by in (1, 2, 3):
            there = moved(spot, axis, by)
            found[axis, by] = (there, device(core, there))
    return found


class Sends:
    def __init__(self, send_sem, recv_sem):
        self.send_sem, self.recv_sem = send_sem, recv_sem
        self.slots, self.open = {}, []

    def copy(self, name, src, dst, target):
        slot = self.slots.setdefault(name, len(self.slots))
        return pltpu.make_async_remote_copy(
            src_ref=src, dst_ref=dst, send_sem=self.send_sem.at[slot], recv_sem=self.recv_sem.at[slot],
            device_id=target, device_id_type=MESH,
        )

    def start(self, name, make):
        self.copy(name, *make()).start()
        self.open.append((name, make))

    def arrived(self, name, ref, target):
        self.copy(name, ref, ref, target).wait_recv()

    def drain(self):
        for name, make in self.open:
            self.copy(name, *make()).wait_send()
        self.open = []


def greet(targets):
    barrier = pltpu.get_barrier_semaphore()
    for target in targets:
        pl.semaphore_signal(barrier, inc=1, device_id=target, device_id_type=MESH)
    pl.semaphore_wait(barrier, len(targets))


class Gather:
    def __init__(self, sends, outs, widths):
        self.sends, self.outs = sends, outs
        self.core, self.spot = position()
        self.other = 1 - self.core
        self.sibling = device(1 - self.core, self.spot)
        self.near = neighbours(self.core, self.spot)
        self.jobs = [
            [(i, part, cols) for part, cols in enumerate(cut(width // 128, 3))] for i, width in enumerate(widths)
        ]
        self.forwards = [[] for _ in widths]

    def peers(self):
        return [self.sibling] + [self.near[a, by][1] for a in range(3) for by in (1, 3)]

    def block(self, i, whole_axes, at, cols, half=None):
        index = [pl.ds(0, 4) if a in whole_axes else pl.ds(at[a], 1) for a in range(3)]
        half = self.core if half is None else half
        return self.outs[i].at[half, index[0], index[1], index[2], :, pl.ds(cols[0], cols[1])]

    def push(self, name, target, *where):
        def make():
            ref = self.block(*where)
            return ref, ref, target

        self.sends.start(name, make)

    def forward(self, name, *where):
        self.push(name, self.sibling, *where)
        self.forwards[where[0]].append((name, where))

    def plan(self, item, phase):
        for i, part, cols in self.jobs[item]:
            axis = (part + phase) % 3
            done = [(part + p) % 3 for p in range(phase)]
            sides = [self.near[axis, by] for by in (1, 3, 2)]
            halves_of = [(cols[0] + at, size) for at, size in cut(cols[1] // 128, 2)]
            yield i, part, cols, done, sides, halves_of

    def begin(self, item, phase):
        for i, part, cols, done, (right, left, _), two in self.plan(item, phase):
            for step, (a, b) in enumerate(((0, 1), (1, 0))):
                self.push((i, part, phase, "r", step), right[1], i, done, self.spot, two[a])
                self.push((i, part, phase, "l", step), left[1], i, done, self.spot, two[b])
            if phase == 2:
                self.forward((i, part, "f"), i, done, self.spot, cols)

    def relay(self, item, phase):
        for i, part, cols, done, (right, left, _), two in self.plan(item, phase):
            for side, source, target, cc in (("r", left, right, two[0]), ("l", right, left, two[1])):
                where = (i, done, source[0], cc)
                self.sends.arrived((i, part, phase, side, 0), self.block(*where), source[1])
                self.push((i, part, phase, side, 2), target[1], *where)
                if phase == 2:
                    self.forward((i, part, "f", side, 0), *where)

    def finish(self, item, phase):
        for i, part, cols, done, (right, left, far), two in self.plan(item, phase):
            for side, step, at, cc, source in (
                ("r", 1, left, two[1], left),
                ("l", 1, right, two[0], right),
                ("r", 2, far, two[0], left),
                ("l", 2, far, two[1], right),
            ):
                where = (i, done, at[0], cc)
                self.sends.arrived((i, part, phase, side, step), self.block(*where), source[1])
                if phase == 2:
                    self.forward((i, part, "f", side, step), *where)

    def received(self, item):
        for name, (i, done, at, cc) in self.forwards[item]:
            self.sends.arrived(name, self.block(i, done, at, cc, self.other), self.sibling)


class Exchange:
    def __init__(self, sends, key, bufs, lanes, jobs):
        self.sends, self.key, self.bufs, self.lanes, self.jobs = sends, key, bufs, lanes, jobs
        self.core, self.spot = position()
        self.other = 1 - self.core
        self.mine, self.theirs = (
            [pl.ds(pl.multiple_of(lane * 256 + core * 128, 128), 128) for lane in range(lanes)]
            for core in (self.core, self.other)
        )
        self.sibling = device(self.other, self.spot)
        self.near = neighbours(self.core, self.spot)

    def index(self, cols, axis=None, where=None):
        return tuple(pl.ds(where, 1) if a == axis else pl.ds(0, 4) for a in range(3)) + (slice(None), cols)

    def moves(self, stage, which):
        before, after = self.bufs[stage], self.bufs[stage + 1]
        away, stay = [], []
        if stage == 0:
            for lane in range(self.lanes):
                mine, theirs = self.index(self.mine[lane]), self.index(self.theirs[lane])
                away.append(((self.key, 0, lane), theirs, mine, self.sibling, theirs, self.sibling))
                stay.append(mine)
            return before, after, away, stay
        for number, (lo, width, first) in enumerate(self.jobs):
            if which is not None and number not in which:
                continue
            axis = (first + stage - 1) % 3
            cols = pl.ds(lo, width)
            here = self.index(cols, axis, self.spot[axis])
            for by in (2, 1, 3):
                there, target = self.near[axis, by]
                behind, source = self.near[axis, 4 - by]
                away.append(
                    (
                        (self.key, stage, number, by),
                        self.index(cols, axis, there[axis]),
                        here,
                        target,
                        self.index(cols, axis, behind[axis]),
                        source,
                    )
                )
            stay.append(here)
        return before, after, away, stay

    def launch(self, stage, which=None):
        before, after, away, stay = self.moves(stage, which)
        for name, src, dst, target, _, _ in away:
            self.sends.start(name, lambda src=src, dst=dst, target=target: (before.at[src], after.at[dst], target))
        for here in stay:
            after[here] = before[here]

    def land(self, stage, which=None):
        _, after, away, _ = self.moves(stage, which)
        for name, _, _, _, landing, source in away:
            self.sends.arrived(name, after.at[landing], source)

    def fill(self, lane, scratch, values):
        row = 0
        for value in values:
            for j in range(value.shape[1] // 128):
                scratch[pl.ds(row, N_DEV, stride=16), :] = value[:, j * 128 : (j + 1) * 128].astype(F32)
                row += 1
        blocks = scratch[...].reshape(4, 4, 4, 2, 16, 128)
        for core in range(2):
            at = lane * 256 + core * 128
            self.bufs[0][:, :, :, :, at : at + 128] = blocks[:, :, :, core].astype(BF)


BY_CORE = [(0, 128, 0), (128, 128, 1)]


WALL = 768
TOKEN_ROWS = 48
WIDTHS = (4 * HCOLS + 7 * AR, D + FB + WALL, FB + WALL, FB + WALL)
FSTEPS = H
BLOCKS = FFP // FB


def forward_kernel(
    split_ref, got_ref, gain1_ref, gain2_ref, mask_ref, place_ref, pers_ref,
    mine0, mine1, mine2, mine3,
    g0_ref, g1_ref, g2_ref, g3_ref, proj_ref, x_ref, h1_ref, lat_ref, wf_ref, lw_ref, back_ref, dz_ref, dmid_ref,
    grads_ref,
    flat, d_ref, dec_ref, dect_ref, inc0, inc1, inc2, inc3, stage0, stage1, stage2, stage3,
    w_buf, up_buf, down_buf, z_ref, wup_buf, wd_buf, lead_buf,
    x2_ref, h2_ref, inv_ref, lat_out_ref, lat_up_ref, dl_down_ref, acc_ref, lat_acc_ref, dh_ref, dlat_ref,
    send_sem, recv_sem, local_sem, w_sem, j_sem,
):
    step = pl.program_id(0)
    mine, inc = (mine0, mine1, mine2, mine3), (inc0, inc1, inc2, inc3)
    stage, outs = (stage0, stage1, stage2, stage3), (g0_ref, g1_ref, g2_ref, g3_ref)
    sends = Sends(send_sem, recv_sem)
    ring = Gather(sends, outs, WIDTHS)
    core, spot = ring.core, ring.spot
    other = 1 - core
    items = range(4)

    def head_loads(h, slot):
        half, place = h // 4, pl.multiple_of((h % 4) * HCOLS, 128)
        return (
            pltpu.make_async_copy(
                g0_ref.at[half, :, :, :, :, pl.ds(place, HCOLS)], w_buf.at[slot], w_sem.at[slot, 0]
            ),
            pltpu.make_async_copy(
                g0_ref.at[1, h // 2, pl.ds(2 * (h % 2), 2), :, :, pl.ds(4 * HCOLS, HCOLS)],
                up_buf.at[slot],
                w_sem.at[slot, 1],
            ),
        )

    def down_load():
        return pltpu.make_async_copy(
            g0_ref.at[0, :, :, :, :, pl.ds(4 * HCOLS, HCOLS)], down_buf, local_sem.at[0]
        )

    def lead_load():
        return pltpu.make_async_copy(g1_ref.at[:, :, :, :, :, pl.ds(0, D)], lead_buf, local_sem.at[0])

    def up_load(k):
        at = D if k == 0 else 0
        return pltpu.make_async_copy(
            outs[k + 1].at[:, :, :, :, :, pl.ds(at, FB)], wup_buf.at[k % 2], j_sem.at[k % 2, 0]
        )

    def wall_load(k):
        at = D + FB if k == 0 else FB
        return pltpu.make_async_copy(
            outs[k + 1].at[:, :, :, :, :, pl.ds(at, WALL)], wd_buf.at[k % 2], j_sem.at[k % 2, 1]
        )

    @pl.when(step == 0)
    def _():
        greet([ring.sibling] + [there[1] for there in ring.near.values()])
        for i in items:
            sends.start(("pair", i), lambda i=i: (mine[i].at[other], inc[i], ring.sibling))
        own_copy = lambda i: pltpu.make_async_copy(
            stage[i], outs[i].at[core, spot[0], spot[1], spot[2]], local_sem.at[i]
        )
        for i in items:
            sends.arrived(("pair", i), inc[i], ring.sibling)
            own, theirs = mine[i][core], inc[i][...]
            first = jnp.where(core == 0, own, theirs)
            last = jnp.where(core == 0, theirs, own)
            stage[i][...] = jnp.concatenate([first, last], axis=0).astype(BF)
            own_copy(i).start()
        for i in items:
            own_copy(i).wait()
            ring.begin(i, 0)
        flat[...] = got_ref[...].astype(F32).reshape(N_DEV * TOKEN_ROWS, 128)

        def columns(first, count):
            return jnp.concatenate(
                [flat[pl.ds(first + c, N_DEV, stride=TOKEN_ROWS), :].astype(BF) for c in range(count)], axis=1
            )

        for i in items:
            ring.relay(i, 0)
        for i in items:
            ring.finish(i, 0)
            ring.begin(i, 1)
        for i in items:
            ring.relay(i, 1)
        ring.finish(0, 1)
        ring.begin(0, 2)
        for i in items[1:]:
            ring.finish(i, 1)
        rates = columns(4 * D // 128, 1)
        for m in range(MB):
            s = slice(m * GROUP, (m + 1) * GROUP)
            x_ref[s, :] = dot(place_ref[m], columns(m * D // 128, D // 128), TN).astype(BF)
            d_ref[s, :] = dot(place_ref[m], columns((MB + m) * D // 128, D // 128), TN).astype(BF)
            sent = rates[:, m * 3 * H : (m + 1) * 3 * H]
            dec_ref[s, :] = dot(place_ref[m], sent, TN)
            dect_ref[:, s] = dot(sent, place_ref[m], TN)
        decay_kernel(split_ref, dec_ref, dect_ref, wf_ref, lw_ref)
        normed, _ = norm_fwd(x_ref[...].astype(F32), gain1_ref[...])
        h1_ref[...] = normed.astype(BF)
        ring.relay(0, 2)
        ring.begin(1, 2)
        ring.finish(0, 2)
        ring.received(0)
        for copy in head_loads(0, 0):
            copy.start()
        down_load().start()
        down_load().wait()
        latent = dot(h1_ref[...], down_buf[...].reshape(D, HCOLS))
        mask = mask_ref[...]
        for part in range(7):
            s = slice(part * AR, (part + 1) * AR)
            lat_ref[:, s] = (latent[:, s] * mask).astype(BF)

    @pl.when(step == 3)
    def _():
        ring.relay(1, 2)
        ring.begin(2, 2)

    @pl.when(step == FSTEPS - 1)
    def _():
        ring.finish(1, 2)
        ring.received(1)
        for copy in (lead_load(), up_load(0), wall_load(0)):
            copy.start()
        ring.relay(2, 2)
        ring.begin(3, 2)

    @pl.when(step < FSTEPS)
    def _():
        slot = step % 2
        for copy in head_loads(step, slot):
            copy.wait()

        @pl.when(step + 1 < FSTEPS)
        def _():
            for copy in head_loads(step + 1, 1 - slot):
                copy.start()

        base = dot(h1_ref[...], w_buf[slot].reshape(D, HCOLS))
        up = up_buf[slot].reshape(HEAD, HCOLS)
        pieces = []
        for part in range(7):
            s = slice(part * AR, (part + 1) * AR)
            piece = base[:, part * HEAD : (part + 1) * HEAD] + dot(lat_ref[:, s], up[:, s], NT)
            proj_ref[:, part * HEAD : (part + 1) * HEAD] = piece
            pieces.append(piece)
        q, k, v = (pieces[i].astype(BF) for i in range(3))
        pk, pv = pers_ref[0, :, pl.ds(pl.multiple_of(step * HEAD, HEAD), HEAD)], pers_ref[
            1, :, pl.ds(pl.multiple_of(step * HEAD, HEAD), HEAD)
        ]
        near, far = attend(q, k, v, pk, pv, allowed_mask(split_ref))
        att = attend_out(near.astype(BF), far.astype(BF), v, pv)
        kn, _ = unit(pieces[3])
        qn, _ = unit(pieces[5])
        here = pl.ds(step, 1)
        mem = memory_out(memory_terms(kn, qn, pieces[4], wf_ref.at[here], lw_ref.at[here]))
        z_ref[:, pl.ds(pl.multiple_of(step * HEAD, HEAD), HEAD)] = (
            att + jax.nn.sigmoid(pieces[6]) * mem
        ).astype(BF)

    lead = lambda half, lo, hi: lead_buf[half, :, :, :, :, lo:hi].reshape(D, hi - lo)
    out_down = lambda: lead(0, 0, 128)
    up_down = lambda: lead(0, 128, 384)
    out_up = lambda: lead(0, 384, 512)
    down_up = lambda: lead(0, 512, 640)
    w_out = lambda: lead(1, 0, D)

    @pl.when(step == FSTEPS)
    def _():
        lead_load().wait()
        mask = mask_ref[...]
        z = z_ref[...]
        lat_out_ref[...] = (dot(z, out_down()) * mask).astype(BF)
        x2 = x_ref[...].astype(F32) + (dot(z, w_out()) + dot(lat_out_ref[...], out_up(), NT))
        x2_ref[...] = x2
        normed, inv = norm_fwd(x2, gain2_ref[...])
        inv_ref[...] = jnp.broadcast_to(inv, inv_ref.shape)
        h2_ref[...] = normed.astype(BF)
        latent = dot(h2_ref[...], up_down())
        lat_up_ref[:, :AR] = (latent[:, :AR] * mask).astype(BF)
        lat_up_ref[:, AR:] = (latent[:, AR:] * mask).astype(BF)
        dl_down_ref[...] = (dot(d_ref[...], down_up()) * mask).astype(BF)
        for ref in (acc_ref, lat_acc_ref, dh_ref, dlat_ref):
            ref[...] = jnp.zeros_like(ref)

    @pl.when(step == FSTEPS)
    def _():
        ring.finish(2, 2)
        ring.received(2)
        up_load(1).start()
        wall_load(1).start()

    @pl.when(step >= FSTEPS)
    def _():
        k = step - FSTEPS
        slot = k % 2
        h2 = h2_ref[...]
        d = d_ref[...]
        lat0, lat1 = lat_up_ref[:, :AR], lat_up_ref[:, AR:]
        wall = lambda half, lo, hi: wd_buf[slot, half, :, :, :, :, lo:hi].reshape(FB, hi - lo)
        pltpu.make_async_copy(wup_buf.at[slot], wup_buf.at[slot], j_sem.at[slot, 0]).wait()
        pltpu.make_async_copy(wd_buf.at[slot], wd_buf.at[slot], j_sem.at[slot, 1]).wait()
        w_gate, w_lift = (wup_buf[slot, half].reshape(D, FB) for half in range(2))
        wda, wdb = wall(0, 0, 768), wall(1, 0, 256)
        uu0, uu1, dd = wall(1, 256, 384), wall(1, 384, 512), wall(1, 512, 640)
        gate = dot(h2, w_gate) + dot(lat0, uu0, NT)
        lift = dot(h2, w_lift) + dot(lat1, uu1, NT)
        sig = jax.nn.sigmoid(gate)
        silu = gate * sig
        act = (silu * lift).astype(BF)
        d_act = dot(d[:, :768], wda, NT) + dot(d[:, 768:], wdb, NT) + dot(dl_down_ref[...], dd, NT)
        d_gate = (d_act * lift * (sig * (1.0 + gate * (1.0 - sig)))).astype(BF)
        d_lift = (d_act * silu).astype(BF)
        acc_ref[:, :768] += dot(act, wda)
        acc_ref[:, 768:] += dot(act, wdb)
        lat_acc_ref[...] += dot(act, dd)
        dh_ref[...] += dot(d_gate, w_gate, NT) + dot(d_lift, w_lift, NT)
        dlat_ref[:, :AR] += dot(d_gate, uu0)
        dlat_ref[:, AR:] += dot(d_lift, uu1)
        for half, at, term in (
            (0, k * 256, dot(d_gate, lat0, TN)),
            (0, k * 256 + AR, dot(d_lift, lat1, TN)),
            (1, k * AR, dot(act, dl_down_ref[...], TN)),
        ):
            at = pl.ds(pl.multiple_of(at, AR), AR)
            grads_ref[half, :, :, at] = term.reshape(64, 16, AR).astype(BF)

        @pl.when(k == 0)
        def _():
            ring.relay(3, 2)

        @pl.when(k == 1)
        def _():
            ring.finish(3, 2)
            ring.received(3)
            up_load(2).start()
            wall_load(2).start()

    @pl.when(step == FSTEPS + BLOCKS - 1)
    def _():
        mask = mask_ref[...]
        lat_down = (lat_acc_ref[...] * mask).astype(BF)
        out = (x2_ref[...] + acc_ref[...] + dot(lat_down, down_up(), NT)).astype(BF)
        for m in range(MB):
            s = slice(m * GROUP, (m + 1) * GROUP)
            back_ref[:, m * D : (m + 1) * D] = dot(place_ref[m], out[s]).astype(BF)
        d = d_ref[...]
        h2 = h2_ref[...]
        z = z_ref[...]

        def put(half, at, value):
            grads_ref[half, :, :, at : at + AR] = value.reshape(64, 16, AR).astype(BF)

        put(0, 768, dot(d, lat_down, TN))
        dlu0 = (dlat_ref[:, :AR] * mask).astype(BF)
        dlu1 = (dlat_ref[:, AR:] * mask).astype(BF)
        put(1, 640, dot(h2, dlu0, TN))
        put(1, 768, dot(h2, dlu1, TN))
        ud = up_down()
        dh = dh_ref[...] + (dot(dlu0, ud[:, :AR], NT) + dot(dlu1, ud[:, AR:], NT))
        dmid = d.astype(F32) + norm_bwd(dh, x2_ref[...], inv_ref[:, :1], gain2_ref[...])
        dmid_ref[...] = dmid
        dmb = dmid.astype(BF)
        dlo = (dot(dmb, out_up()) * mask).astype(BF)
        put(1, 384, dot(z, dlo, TN))
        put(1, 512, dot(dmb, lat_out_ref[...], TN))
        dz_ref[...] = (dot(dmb, w_out(), NT) + dot(dlo, out_down(), NT)).astype(BF)
        sends.drain()


def forward_call(split, got, gain1, gain2, mask, place, persistent, mine):
    once = pl.Buffered(1)
    whole = lambda *shape: pl.BlockSpec(shape, lambda s: (0,) * len(shape), pipeline_mode=once)
    hbm = pl.BlockSpec(memory_space=pl.ANY)
    slots = 4 * (1 + 3 * (3 * 6 + 7))
    return pl.pallas_call(
        forward_kernel,
        grid=(FSTEPS + BLOCKS,),
        out_shape=tuple(jax.ShapeDtypeStruct((2, 4, 4, 4, 16, width), BF) for width in WIDTHS)
        + (
            jax.ShapeDtypeStruct((ROWS, 7 * D), F32),
            jax.ShapeDtypeStruct((ROWS, D), BF),
            jax.ShapeDtypeStruct((ROWS, D), BF),
            jax.ShapeDtypeStruct((ROWS, 7 * AR), BF),
            jax.ShapeDtypeStruct((H, MB, GROUP, GROUP), F32),
            jax.ShapeDtypeStruct((H, MB, 8, GROUP), F32),
            jax.ShapeDtypeStruct((GROUP, MB * D), BF),
            jax.ShapeDtypeStruct((ROWS, D), BF),
            jax.ShapeDtypeStruct((ROWS, D), F32),
            jax.ShapeDtypeStruct((2, 64, 16, 896), BF),
        ),
        in_specs=[
            pl.BlockSpec(memory_space=pltpu.SMEM),
            whole(N_DEV, TOKEN_ROWS, 128),
            whole(1, D),
            whole(1, D),
            whole(ROWS, AR),
            whole(MB, GROUP, GROUP),
            whole(2, NP, D),
        ]
        + [whole(2, 8, width) for width in WIDTHS],
        out_specs=(hbm,) * 4
        + (
            pl.BlockSpec((ROWS, HCOLS), lambda s: (0, jnp.minimum(s, FSTEPS - 1))),
            whole(ROWS, D),
            whole(ROWS, D),
            whole(ROWS, 7 * AR),
            whole(H, MB, GROUP, GROUP),
            whole(H, MB, 8, GROUP),
            whole(GROUP, MB * D),
            whole(ROWS, D),
            whole(ROWS, D),
            whole(2, 64, 16, 896),
        ),
        scratch_shapes=[
            pltpu.VMEM((N_DEV * TOKEN_ROWS, 128), F32),
            pltpu.VMEM((ROWS, D), BF),
            pltpu.VMEM((ROWS, 3 * H), F32),
            pltpu.VMEM((3 * H, ROWS), F32),
        ]
        + [pltpu.VMEM((8, width), F32) for width in WIDTHS]
        + [pltpu.VMEM((16, width), BF) for width in WIDTHS]
        + [
            pltpu.VMEM((2, 4, 4, 4, 16, HCOLS), BF),
            pltpu.VMEM((2, 2, 4, 16, HCOLS), BF),
            pltpu.VMEM((4, 4, 4, 16, HCOLS), BF),
            pltpu.VMEM((ROWS, D), BF),
            pltpu.VMEM((2, 2, 4, 4, 4, 16, FB), BF),
            pltpu.VMEM((2, 2, 4, 4, 4, 16, WALL), BF),
            pltpu.VMEM((2, 4, 4, 4, 16, D), BF),
            pltpu.VMEM((ROWS, D), F32),
            pltpu.VMEM((ROWS, D), BF),
            pltpu.VMEM((ROWS, 128), F32),
            pltpu.VMEM((ROWS, AR), BF),
            pltpu.VMEM((ROWS, 2 * AR), BF),
            pltpu.VMEM((ROWS, AR), BF),
            pltpu.VMEM((ROWS, D), F32),
            pltpu.VMEM((ROWS, AR), F32),
            pltpu.VMEM((ROWS, D), F32),
            pltpu.VMEM((ROWS, 2 * AR), F32),
            pltpu.SemaphoreType.DMA((slots,)),
            pltpu.SemaphoreType.DMA((slots,)),
            pltpu.SemaphoreType.DMA((4,)),
            pltpu.SemaphoreType.DMA((2, 2)),
            pltpu.SemaphoreType.DMA((2, 2)),
        ],
        compiler_params=pltpu.CompilerParams(
            collective_id=0, has_side_effects=True, vmem_limit_bytes=VMEM_LIMIT
        ),
        name="gather_forward",
    )(split, got, gain1, gain2, mask, place, persistent, *mine)


class Scatter:
    def __init__(self, sends, key, grads, out, inc0, total, inc1, inc2, inc3, t1, t2):
        self.sends, self.key, self.grads, self.out = sends, key, grads, out
        self.inc0, self.total, self.inc = inc0, total, (None, inc1, inc2, inc3)
        self.t1, self.t2 = t1, t2
        self.core, self.spot = position()
        self.other = 1 - self.core
        self.sibling = device(1 - self.core, self.spot)
        self.near = neighbours(self.core, self.spot)
        self.parts = [(part, pl.ds(*cols)) for part, cols in enumerate(cut(7, 3))]

    def peers(self):
        return [self.sibling] + [there[1] for there in self.near.values()]

    def pair(self):
        for x in range(4):
            self.sends.start(
                (self.key, "pair", x),
                lambda x=x: (
                    self.grads.at[self.other, pl.ds(16 * x, 16)],
                    self.inc0.at[x],
                    self.sibling,
                ),
            )

    def source(self, phase, part, at):
        axis = (part + phase - 1) % 3
        cs = self.parts[part][1]
        if phase == 1:
            index = tuple(at if a == axis else slice(None) for a in range(3))
            return self.total, index + (slice(None), cs)
        rest = [a for a in range(3) if a != part]
        if phase == 2:
            index = (at, slice(None)) if rest[0] == axis else (slice(None), at)
            return self.t1, index + (slice(None), cs)
        return self.t2, (at, slice(None), cs)

    def landing(self, phase, part, k):
        return (k,) + (slice(None),) * (4 - phase) + (self.parts[part][1],)

    def send(self, phase):
        for part, _ in self.parts:
            axis = (part + phase - 1) % 3
            for k, by in enumerate((2, 1, 3)):
                to = self.near[axis, by]

                def make(part=part, axis=axis, to=to, k=k):
                    ref, index = self.source(phase, part, to[0][axis])
                    return ref.at[index], self.inc[phase].at[self.landing(phase, part, k)], to[1]

                self.sends.start((self.key, part, phase, by), make)

    def add(self, phase):
        for part, cs in self.parts:
            axis = (part + phase - 1) % 3
            ref, index = self.source(phase, part, self.spot[axis])
            acc = ref[index].astype(F32)
            for k, by in enumerate((2, 1, 3)):
                here = self.landing(phase, part, k)
                source = self.near[axis, 4 - by][1]
                self.sends.arrived((self.key, part, phase, by), self.inc[phase].at[here], source)
                acc = acc + self.inc[phase][here].astype(F32)
            if phase == 1:
                self.t1[:, :, :, cs] = acc.astype(BF)
            elif phase == 2:
                self.t2[:, :, cs] = acc.astype(BF)
            else:
                self.out[self.core, :, cs] = acc

    def add_pair(self):
        for x in range(4):
            self.sends.arrived((self.key, "pair", x), self.inc0.at[x], self.sibling)
            both = self.grads[self.core, pl.ds(16 * x, 16)].astype(F32) + self.inc0[x].astype(F32)
            self.total[x] = both.reshape(4, 4, 16, 896).astype(BF)

    def swap(self):
        self.sends.start(
            (self.key, "last"), lambda: (self.out.at[self.core], self.out.at[self.core], self.sibling)
        )

    def swapped(self):
        self.sends.arrived((self.key, "last"), self.out.at[self.other], self.sibling)


def backward_kernel(
    split_ref, x_ref, gain_ref, mask_ref, place_ref, proj_ref, dz_ref, dmid_ref, h1_ref, lat_ref,
    w_ref, down_ref, up_ref, pers_ref, wf_ref, lw_ref, ffn_ref, back_ref,
    act_out, grad_out, ffn_out, heads_out,
    dh_ref, dlat_ref, dlat_half, dy_ref, grads_ref, *rest,
):
    step = pl.program_id(0)
    send_sem, recv_sem = rest[-2:]
    sends = Sends(send_sem, recv_sem)
    first_sums = Scatter(sends, 0, ffn_ref, *rest[:8])
    last_sums = Scatter(sends, 1, grads_ref, *rest[8:16])
    flat = rest[26]
    ex_act = Exchange(sends, "a", rest[16:21], 1, BY_CORE)
    ex_grad = Exchange(sends, "g", rest[21:26], 1, BY_CORE)

    def one_head():
        pieces = [proj_ref[:, p * HEAD : (p + 1) * HEAD] for p in range(7)]
        q, k, v = (pieces[i].astype(BF) for i in range(3))
        pk, pv = pers_ref[0], pers_ref[1]
        near, far = attend(q, k, v, pk, pv, allowed_mask(split_ref))
        near_half = near.astype(BF)
        dz = dz_ref[...]
        d_near = by_group(lambda s, g: dot(dz[s], v[s], NT))
        d_far = dot(dz, pv, NT)
        d_v = by_group(lambda s, g: dot(near_half[s], dz[s], TN))
        total = jnp.sum(d_near * near, axis=-1, keepdims=True) + jnp.sum(
            d_far * far, axis=-1, keepdims=True
        )
        ds_near = (near * (d_near - total) * SCALE).astype(BF)
        ds_far = (far * (d_far - total) * SCALE).astype(BF)
        d_q = by_group(lambda s, g: dot(ds_near[s], k[s])) + dot(ds_far, pk)
        d_k = by_group(lambda s, g: dot(ds_near[s], q[s], TN))

        dzf = dz.astype(F32)
        opening = jax.nn.sigmoid(pieces[6])
        kn, k_inv = unit(pieces[3])
        qn, q_inv = unit(pieces[5])
        kept = memory_terms(kn, qn, pieces[4], wf_ref, lw_ref, plain, dot1)
        mem = memory_out(kept, dot1)
        d_open = dzf * mem * (opening * (1.0 - opening))
        d_kn, d_qn, d_mv = memory_bwd(kept, dzf * opening)
        d_mk = unit_bwd(d_kn, pieces[3], k_inv)
        d_mq = unit_bwd(d_qn, pieces[5], q_inv)
        dy = [item.astype(BF) for item in (d_q, d_k, d_v, d_mk, d_mv, d_mq, d_open)]
        dy_ref[step] = jnp.concatenate(dy, axis=1)
        first = pl.multiple_of(step * 8, 8)
        for part in range(7):
            s = slice(part * AR, (part + 1) * AR)
            dlat_ref[:, s] += dot(dy[part], up_ref[0, :, s])
            grads_ref[1, pl.ds(first, 8), :, s] = (
                dot(dy[part], lat_ref[:, s], TN).reshape(8, 16, AR).astype(BF)
            )

    @pl.when(step == 0)
    def _():
        greet(first_sums.peers())
        ex_act.fill(0, flat, [back_ref[...]])
        ex_act.launch(0)
        first_sums.pair()
        dlat_ref[...] = jnp.zeros_like(dlat_ref)

    @pl.when(step == 1)
    def _():
        ex_act.land(0)
        ex_act.launch(1)

    @pl.when(step == 2)
    def _():
        first_sums.add_pair()
        first_sums.send(1)

    @pl.when(step == 3)
    def _():
        ex_act.land(1)
        ex_act.launch(2)

    @pl.when(step == 5)
    def _():
        first_sums.add(1)
        first_sums.send(2)
        ex_act.land(2)
        ex_act.launch(3)

    @pl.when(step == 6)
    def _():
        first_sums.add(2)
        first_sums.send(3)

    @pl.when(step == 7)
    def _():
        first_sums.add(3)
        first_sums.swap()
        ex_act.land(3)
        act_out[...] = ex_act.bufs[4][...]

    @pl.when(step < H)
    def _():
        one_head()

    @pl.when(step == H)
    def _():
        mask = mask_ref[...]
        for p in range(7):
            s = slice(p * AR, (p + 1) * AR)
            dlat_half[:, s] = (dlat_ref[:, s] * mask).astype(BF)
        grads_ref[0] = dot(h1_ref[...], dlat_half[...], TN).reshape(64, 16, 7 * AR).astype(BF)
        last_sums.pair()
        dh_ref[...] = dot(dlat_half[...], down_ref[0], NT)

    @pl.when(step == H + 2)
    def _():
        last_sums.add_pair()
        last_sums.send(1)

    @pl.when(step >= H)
    def _():
        dh_ref[...] += dot(dy_ref[step - H], w_ref[0], NT)

    @pl.when(step == 2 * H - 1)
    def _():
        x = x_ref[...].astype(F32)
        inv = lax.rsqrt(jnp.mean(x * x, axis=-1, keepdims=True) + EPS)
        dx = (dmid_ref[...] + norm_bwd(dh_ref[...], x, inv, gain_ref[...])).astype(BF)
        ex_grad.fill(
            0, flat, [dot(place_ref[m], dx[m * GROUP : (m + 1) * GROUP]) for m in range(MB)]
        )
        ex_grad.launch(0)
        first_sums.swapped()
        ffn_out[...] = first_sums.out[...]
        ex_grad.land(0)
        ex_grad.launch(1)
        last_sums.add(1)
        last_sums.send(2)
        ex_grad.land(1)
        ex_grad.launch(2)
        last_sums.add(2)
        last_sums.send(3)
        ex_grad.land(2)
        ex_grad.launch(3)
        last_sums.add(3)
        last_sums.swap()
        ex_grad.land(3)
        grad_out[...] = ex_grad.bufs[4][...]
        last_sums.swapped()
        heads_out[...] = last_sums.out[...]
        sends.drain()


def backward_call(split, x, gain, mask, place, proj, dz, dmid, h1, lat, a1, persistent, wf, lw, grads_ffn, back):
    once = pl.Buffered(1)
    whole = lambda *shape: pl.BlockSpec(shape, lambda s: (0,) * len(shape), pipeline_mode=once)
    head = lambda s: jnp.minimum(s, H - 1)
    late = lambda s: jnp.maximum(s - H, 0)
    buffers = [
        pltpu.VMEM((2, 16, 896), F32),
        pltpu.VMEM((4, 16, 16, 896), BF),
        pltpu.VMEM((4, 4, 4, 16, 896), BF),
        pltpu.VMEM((3, 4, 4, 16, 896), BF),
        pltpu.VMEM((3, 4, 16, 896), BF),
        pltpu.VMEM((3, 16, 896), BF),
        pltpu.VMEM((4, 4, 16, 896), BF),
        pltpu.VMEM((4, 16, 896), BF),
    ]
    slots = 2 * (4 + 3 * 9 + 1) + 2 * (1 + 3 * 6)
    return pl.pallas_call(
        backward_kernel,
        grid=(2 * H,),
        out_shape=(
            jax.ShapeDtypeStruct((4, 4, 4, 16, 256), BF),
            jax.ShapeDtypeStruct((4, 4, 4, 16, 256), BF),
            jax.ShapeDtypeStruct((2, 16, 896), F32),
            jax.ShapeDtypeStruct((2, 16, 896), F32),
        ),
        in_specs=[
            pl.BlockSpec(memory_space=pltpu.SMEM),
            whole(ROWS, D),
            whole(1, D),
            whole(ROWS, AR),
            whole(MB, GROUP, GROUP),
            pl.BlockSpec((ROWS, HCOLS), lambda s: (0, head(s))),
            pl.BlockSpec((ROWS, HEAD), lambda s: (0, head(s))),
            whole(ROWS, D),
            whole(ROWS, D),
            whole(ROWS, 7 * AR),
            pl.BlockSpec((1, D, HCOLS), lambda s: (late(s) // 4, 0, late(s) % 4)),
            pl.BlockSpec((1, D, HCOLS), lambda s: (0, 0, 4), pipeline_mode=once),
            pl.BlockSpec((1, HEAD, HCOLS), lambda s: (1, head(s), 4)),
            pl.BlockSpec((2, NP, HEAD), lambda s: (0, 0, head(s))),
            pl.BlockSpec((1, MB, GROUP, GROUP), lambda s: (head(s), 0, 0, 0)),
            pl.BlockSpec((1, MB, 8, GROUP), lambda s: (head(s), 0, 0, 0)),
            pl.BlockSpec(memory_space=pltpu.VMEM),
            pl.BlockSpec(memory_space=pltpu.VMEM),
        ],
        out_specs=(
            whole(4, 4, 4, 16, 256),
            whole(4, 4, 4, 16, 256),
            pl.BlockSpec(memory_space=pltpu.VMEM),
            pl.BlockSpec(memory_space=pltpu.VMEM),
        ),
        scratch_shapes=[
            pltpu.VMEM((ROWS, D), F32),
            pltpu.VMEM((ROWS, 7 * AR), F32),
            pltpu.VMEM((ROWS, 7 * AR), BF),
            pltpu.VMEM((H, ROWS, HCOLS), BF),
            pltpu.VMEM((2, 64, 16, 896), BF),
        ]
        + buffers * 2
        + [pltpu.VMEM((4, 4, 4, 16, 256), BF)] * 10
        + [pltpu.VMEM((16 * N_DEV, 128), F32)]
        + [pltpu.SemaphoreType.DMA((slots,)), pltpu.SemaphoreType.DMA((slots,))],
        compiler_params=pltpu.CompilerParams(
            collective_id=1, has_side_effects=True, vmem_limit_bytes=VMEM_LIMIT
        ),
        name="backward_scatter",
    )(split, x, gain, mask, place, proj, dz, dmid, h1, lat, a1, a1, a1, persistent, wf, lw, grads_ffn, back)


def selector(parts):
    rows = lax.broadcasted_iota(jnp.int32, (parts * R, parts * AR), 0)
    cols = lax.broadcasted_iota(jnp.int32, (parts * R, parts * AR), 1)
    return (rows // R == cols // AR) & (rows % R == cols % R)


def adapter_of(shape):
    return (lax.broadcasted_iota(jnp.int32, shape, len(shape) - 1) % AR) // R


def pack_kernel(
    lengths_ref, ids_ref, route_ref, tok_ref, cot_ref, decays_ref,
    w_in, w_out, w_up, w_down, in_down, in_up, out_down, out_up, up_down, up_up, down_down, down_up,
    got_ref, item0, item1, item2, item3, to_ref, place_ref, mask_ref, split_ref,
    flat, wide, sent, send_sem, recv_sem, own_sem,
):
    me = lax.axis_index("fsdp")
    barrier = pltpu.get_barrier_semaphore()

    def signal(k, carry):
        pl.semaphore_signal(barrier, inc=1, device_id=((me + k) % N_DEV,), device_id_type=MESH)
        return carry

    lax.fori_loop(1, N_DEV, signal, 0)

    below = lax.broadcasted_iota(jnp.int32, (GROUP, GROUP), 0)
    along = lax.broadcasted_iota(jnp.int32, (GROUP, GROUP), 1)
    for m in range(MB):
        to = (below == route_ref[m, pl.ds(me, 1), :] // GROUP).astype(BF)
        to_ref[m] = to
        for ref, first in ((tok_ref, m * 8), (cot_ref, (MB + m) * 8)):
            value = dot(to, ref[m])
            for j in range(8):
                flat[pl.ds(first + j, N_DEV, stride=TOKEN_ROWS), :] = value[:, j * 128 : (j + 1) * 128]
    rates = [dot(to_ref[m], decays_ref[m], NT) for m in range(MB)]
    rates = jnp.concatenate(rates + [jnp.zeros((GROUP, 128 - MB * 3 * H), F32)], axis=1)
    flat[pl.ds(4 * D // 128, N_DEV, stride=TOKEN_ROWS), :] = rates
    for j in range(4 * D // 128 + 1, TOKEN_ROWS):
        flat[pl.ds(j, N_DEV, stride=TOKEN_ROWS), :] = jnp.zeros((N_DEV, 128), F32)
    sent[...] = flat[...].reshape(N_DEV, TOKEN_ROWS, 128).astype(BF)

    def copy(k):
        target = (me + k) % N_DEV
        return pltpu.make_async_remote_copy(
            src_ref=sent.at[target], dst_ref=got_ref.at[me], send_sem=send_sem.at[k], recv_sem=recv_sem.at[k],
            device_id=(target,), device_id_type=MESH,
        )

    def begin(k, carry):
        copy(k).start()
        return carry

    def end(k, carry):
        copy(k).wait()
        return carry

    pl.semaphore_wait(barrier, N_DEV - 1)
    lax.fori_loop(1, N_DEV, begin, 0)
    own = pltpu.make_async_copy(sent.at[me], got_ref.at[me], own_sem)
    own.start()
    for m in range(MB):
        blocks = route_ref[m]
        landing = jnp.sum(jnp.where(blocks // GROUP == me, blocks % GROUP, 0), axis=1, keepdims=True)
        place_ref[m] = (landing == along).astype(BF)
        early = lengths_ref[m, 0]
        row = lax.broadcasted_iota(jnp.int32, (GROUP, AR), 0)
        adapter = jnp.where(row < early, ids_ref[m, 0], ids_ref[m, 1])
        mask_ref[m * GROUP : (m + 1) * GROUP, :] = (adapter == adapter_of((GROUP, AR))).astype(F32)
        split_ref[m] = jnp.where(early < GROUP, 1.0, 0.0)

    select = selector(7).astype(BF)
    items = (item1, item2, item3)

    def ranks(ref, parts):
        cut_to = select[: parts * R, : parts * AR]
        rows = ref.shape[1]
        out = jnp.zeros((rows, parts * AR), F32)
        for a in range(NAD):
            out = out + jnp.where(adapter_of(out.shape) == a, dot(ref[a], cut_to), 0.0)
        return out

    def ranks_t(ref, parts):
        cut_to = select[: parts * R, : parts * AR]
        cols = ref.shape[2]
        out = jnp.zeros((cols, parts * AR), F32)
        for a in range(NAD):
            out = out + jnp.where(adapter_of(out.shape) == a, dot(ref[a], cut_to, TN), 0.0)
        return out

    def ranks_mid(ref, parts):
        rows = ref.shape[0]
        value = ref[...].astype(F32).reshape(rows * NAD, parts * R).astype(BF)
        value = dot(value, select[: parts * R, : parts * AR]).reshape(rows, NAD, parts * AR)
        mine = adapter_of(value.shape) == lax.broadcasted_iota(jnp.int32, value.shape, 1)
        return jnp.sum(jnp.where(mine, value, 0.0), axis=1)

    def tall(value):
        return jnp.concatenate([value, jnp.zeros((FF_PAD - FF_SHARD, value.shape[1]), F32)], axis=0)

    for h in range(H):
        for part in range(7):
            at = (h % 4) * HCOLS + part * HEAD
            item0[h // 4, :, at : at + HEAD] = w_in[:, part * D + h * HEAD : part * D + (h + 1) * HEAD].astype(F32)
    item0[0, :, 4 * HCOLS :] = ranks(in_down, 7)
    item0[1, :, 4 * HCOLS :] = ranks(in_up, 7)

    item1[0, :, 0:128] = ranks(out_down, 1)
    item1[0, :, 128:384] = ranks(up_down, 2)
    item1[0, :, 384:512] = ranks(out_up, 1)
    item1[0, :, 512:640] = ranks(down_up, 1)
    item1[0, :, 640:D] = jnp.zeros((8, D - 640), F32)
    item1[1, :, 0:D] = w_out[...].astype(F32)

    wide[...] = w_up[...].astype(F32)
    span = 8 * FF_SHARD
    rows = lax.broadcasted_iota(jnp.int32, (span, 3 * 64), 0)
    cols = lax.broadcasted_iota(jnp.int32, (span, 3 * 64), 1)
    unit_at = (cols // 64) * 8 + cols % 8
    spread = ((rows == (cols % 64) // 8 * FF_SHARD + unit_at) & (unit_at < FF_SHARD)).astype(BF)
    pieces = [wide[:, c * span : (c + 1) * span] for c in range(32)]
    moved_up = dot(jnp.concatenate(pieces, axis=0).astype(BF), spread)
    for c in range(32):
        half, chunk = c // 16, c % 16
        for k in range(3):
            at = (D if k == 0 else 0) + chunk * 64
            items[k][half, :, at : at + 64] = moved_up[c * 8 : (c + 1) * 8, k * 64 : (k + 1) * 64]
    down = tall(w_down[...].astype(F32))
    uu, dd = tall(ranks_mid(up_up, 2)), tall(ranks_t(down_down, 1))
    for k in range(3):
        at = (D if k == 0 else 0) + FB
        s = slice(k * 8, (k + 1) * 8)
        items[k][0, :, at : at + 768] = down[s, :768]
        items[k][1, :, at : at + 256] = down[s, 768:]
        items[k][1, :, at + 256 : at + 512] = uu[s]
        items[k][1, :, at + 512 : at + 640] = dd[s]
        items[k][1, :, at + 640 : at + 768] = jnp.zeros((8, 128), F32)

    own.wait()
    lax.fori_loop(1, N_DEV, end, 0)


def pack_call(lengths, ids, route, tokens, cotangent, decays, weights):
    smem, vmem = pl.BlockSpec(memory_space=pltpu.SMEM), pl.BlockSpec(memory_space=pltpu.VMEM)
    return pl.pallas_call(
        pack_kernel,
        out_shape=(jax.ShapeDtypeStruct((N_DEV, TOKEN_ROWS, 128), BF),)
        + tuple(jax.ShapeDtypeStruct((2, 8, width), F32) for width in WIDTHS)
        + (
            jax.ShapeDtypeStruct((MB, GROUP, GROUP), BF),
            jax.ShapeDtypeStruct((MB, GROUP, GROUP), BF),
            jax.ShapeDtypeStruct((ROWS, AR), F32),
            jax.ShapeDtypeStruct((MB,), F32),
        ),
        in_specs=[smem] * 2 + [vmem] * (4 + len(weights)),
        out_specs=(pl.BlockSpec(memory_space=pl.ANY),) + (vmem,) * 7 + (smem,),
        scratch_shapes=[
            pltpu.VMEM((N_DEV * TOKEN_ROWS, 128), F32),
            pltpu.VMEM((8, 2 * FF), F32),
            pltpu.VMEM((N_DEV, TOKEN_ROWS, 128), BF),
            pltpu.SemaphoreType.DMA((N_DEV,)),
            pltpu.SemaphoreType.DMA((N_DEV,)),
            pltpu.SemaphoreType.DMA,
        ],
        compiler_params=pltpu.CompilerParams(
            collective_id=2, has_side_effects=True, vmem_limit_bytes=VMEM_LIMIT
        ),
        name="pack",
    )(lengths, ids, route, tokens, cotangent, decays, *weights)


def unpack_kernel(
    core_ref, to_ref, act_ref, grad_ref, ffn_ref, heads_ref,
    out_ref, back_ref, in_down, in_up, out_down, out_up, up_down, up_up, down_down, down_up,
    flat,
):
    core = core_ref[0]
    for source, target in ((act_ref, out_ref), (grad_ref, back_ref)):
        got = [source[:, :, :, :, c * 128 : (c + 1) * 128].astype(F32) for c in range(2)]
        flat[...] = jnp.stack(got, axis=3).reshape(16 * N_DEV, 128)
        for m in range(MB):
            value = jnp.concatenate(
                [flat[pl.ds(m * 8 + j, N_DEV, stride=16), :].astype(BF) for j in range(8)], axis=1
            )
            target[m] = dot(to_ref[m], value, TN).astype(BF)
    own = pl.ds(pl.multiple_of(core * 8, 8), 8)
    heads = [heads_ref[half, own, :] for half in range(2)]
    ffn = [ffn_ref[half, own, :] for half in range(2)]
    select = selector(7).astype(F32)

    def tall(value, width):
        return jnp.concatenate([value[:, k * width : (k + 1) * width] for k in range(3)], axis=0)

    def put(ref, value, parts):
        rows, width = value.shape
        shape = (NAD, rows, width)
        mine = adapter_of(shape) == lax.broadcasted_iota(jnp.int32, shape, 0)
        apart = jnp.where(mine, value[None], 0.0).reshape(NAD * rows, width)
        ref[...] = exact(apart, select[: parts * R, :width], NT).reshape(NAD, rows, parts * R)

    put(in_down, heads[0], 7)
    put(in_up, heads[1], 7)
    put(out_down, ffn[1][:, 384:512], 1)
    put(out_up, ffn[1][:, 512:640], 1)
    put(up_down, ffn[1][:, 640:896], 2)
    put(down_up, ffn[0][:, 768:], 1)
    value = tall(ffn[0][:, :768], 256)
    shape = (FF_PAD, NAD, 2 * AR)
    mine = adapter_of(shape) == lax.broadcasted_iota(jnp.int32, shape, 1)
    apart = jnp.where(mine, jnp.broadcast_to(value[:, None, :], shape), 0.0).reshape(FF_PAD * NAD, 2 * AR)
    up_up[...] = exact(apart, select[: 2 * R, : 2 * AR], NT).reshape(FF_PAD, NAD, 2 * R)[:FF_SHARD]
    value = tall(ffn[1][:, :384], AR)
    for a in range(NAD):
        mine = jnp.where(adapter_of(value.shape) == a, value, 0.0)
        down_down[a] = exact(select[:R, :AR], mine, NT)[:, :FF_SHARD]


def unpack_call(core, to, act, grad, ffn_sums, heads_sums, shapes):
    smem, vmem = pl.BlockSpec(memory_space=pltpu.SMEM), pl.BlockSpec(memory_space=pltpu.VMEM)
    return pl.pallas_call(
        unpack_kernel,
        out_shape=(jax.ShapeDtypeStruct((MB, GROUP, D), BF),) * 2
        + tuple(jax.ShapeDtypeStruct(shape, F32) for shape in shapes),
        in_specs=[smem] + [vmem] * 5,
        out_specs=(vmem,) * (2 + len(shapes)),
        scratch_shapes=[pltpu.VMEM((16 * N_DEV, 128), F32)],
        compiler_params=pltpu.CompilerParams(vmem_limit_bytes=VMEM_LIMIT),
        name="unpack",
    )(core, to, act, grad, ffn_sums, heads_sums)


def body(
    tokens, cotangent, decays, route, lengths, adapter_ids, gain_mix, gain_ffn, persistent,
    w_in, w_out, w_up, w_down, in_down, in_up, out_down, out_up, up_down, up_up, down_down, down_up,
):
    me = lax.axis_index("fsdp").astype(jnp.int32)
    weights = (
        w_in, w_out, w_up, w_down, in_down, in_up, out_down, out_up, up_down, up_up, down_down, down_up,
    )
    turned = lambda value: jnp.swapaxes(value, 1, 2)
    views = (None,) * 5 + (turned, None, turned, None, lambda value: value.transpose(2, 0, 1), turned, turned)
    back_views = views[:9] + (lambda value: value.transpose(1, 2, 0), turned, turned)
    viewed = [item if view is None else view(item) for item, view in zip(weights, views)]
    got, *items, to, place, mask, split = pack_call(
        lengths[:, 0], adapter_ids[:, 0], route.reshape(MB, N_DEV, GROUP), tokens, cotangent, turned(decays), viewed
    )
    gain_mix, gain_ffn = gain_mix[None, :], gain_ffn[None, :]
    a1, _, _, _, proj, x, h1, lat, wf, lw, back, dz, dmid, grads_ffn = forward_call(
        split, got, gain_mix, gain_ffn, mask, place, persistent, items
    )
    act, grad, ffn_sums, heads_sums = backward_call(
        split, x, gain_mix, mask, place, proj, dz, dmid, h1, lat, a1.reshape(2, D, WIDTHS[0]), persistent, wf, lw,
        grads_ffn, back,
    )
    outs = unpack_call((me % 2)[None], to, act, grad, ffn_sums, heads_sums, [item.shape for item in viewed[4:]])
    grads = [item if view is None else view(item) for item, view in zip(outs[2:], back_views[4:])]
    return tuple(outs[:2]) + tuple(grads)


def solution(mesh):
    rows, cols = P(None, "fsdp", None), P(None, None, "fsdp")
    weight = P("fsdp", None)
    return jax.shard_map(
        body,
        mesh=mesh,
        in_specs=(rows, rows, rows, P(), rows, rows, P(), P(), P())
        + (weight,) * 4
        + (rows, cols) * 4,
        out_specs=(rows, rows) + (rows, cols) * 4,
        check_vma=False,
    )
```

profile of v0, /device:TPU:1, one launch (start us, length us, event | category | flops | bytes accessed | tf_op | source)
XLA Modules:
  0.0 247.6 jit_solution(12181011085279686449)
XLA Ops:
  0.6 1.6 copy.33
  2.2 39.6 %pack.1 = (bf16[128,48,128]{2,1,0:T(8,128)(2,1)}, f32[2,8,4480]{2,1,0:T(8,128)}, f32[2,8,2816]{2,1,0:T(8,128)}, f32[2,8,1792]{2,1,0:T(8,128)}, f32[2,8,1792]{2,1...) custom-call(s32[2,2]{1,0:T(2,128)} %bitcast.35, ...), custom_call_target="tpu_custom_call" | custom-call | tf_op jit(solution)/shard_map/pack/pallas_call | solution.py:1215
  41.8 133.9 %gather_forward.1 = (bf16[2,4,4,4,16,4480]{5,4,3,2,1,0:T(8,128)(2,1)}, bf16[2,4,4,4,16,2816]{5,4,3,2,1,0:T(8,128)(2,1)}, bf16[2,4,4,4,16,1792]{5,4,3,2,1,0:T(8,1...) custom-call(f32[2]{0:T(128)} %get-tuple-element.45.split_ref, ...), custom_call_target="tpu_custom_call" | custom-call | tf_op jit(solution)/shard_map/gather_forward/pallas_call | solution.py:693
  175.7 68.0 %backward_scatter.1 = (bf16[4,4,4,16,256]{4,3,2,1,0:T(8,128)(2,1)}, bf16[4,4,4,16,256]{4,3,2,1,0:T(8,128)(2,1)}, f32[2,16,896]{2,1,0:T(8,128)}, f32[2,16,896]{2,1,0:T(8,128)}) custom-call(f32[2]{0:T(128)} %get-tuple-element.45.split_ref, bf16[256,1024]{1,0:T(8,128)(2,1)} %get-tuple-element.53.x_ref, f32[1,1024]{1,0:T(1,128)} %bitcast.32, ...), custom_call_target="tpu_custom_call" | custom-call | tf_op jit(solution)/shard_map/backward_scatter/pallas_call | solution.py:1019
  243.7 4.0 %unpack.1 = (bf16[2,128,1024]{2,1,0:T(8,128)(2,1)}, bf16[2,128,1024]{2,1,0:T(8,128)(2,1)}, f32[8,8,112]{2,1,0:T(8,128)}, f32[8,8,112]{2,1,0:T(8,128)}, f32[8,8,1...) custom-call(s32[1]{0:T(128)} %bitcast.core_ref, ...), custom_call_target="tpu_custom_call" | custom-call | tf_op jit(solution)/shard_map/unpack/pallas_call | solution.py:1290
where the time goes:
time: 248 us
  Pallas kernels  245 us (99%)
    pallas_call x1, Pallas kernels, forward_call(): pl.pallas_call(forward_kernel, grid=(FSTEPS + BLOCKS,), out_shape=tuple((...  134 us
    pallas_call x1, Pallas kernels, backward_call(): pl.pallas_call(backward_kernel, grid=(2 * H,), out_shape=(jax.ShapeDtypeS...  68 us
    pallas_call x1, Pallas kernels, pack_call(): pl.pallas_call(pack_kernel, out_shape=(jax.ShapeDtypeStruct((N_DEV, TOKEN...  39.6 us

commit v1 on v0

--- a/solution.py
+++ b/solution.py
@@ -210,11 +210,11 @@
     return tuple((v + by + 4) % 4 if i == axis else v for i, v in enumerate(spot))
 
 
-def cut(lanes, count):
+def cut(lanes, count, first=0):
     base, extra = divmod(lanes, count)
     runs, at = [], 0
     for i in range(count):
-        size = base + (1 if i < extra else 0)
+        size = base + (1 if (i - first) % count < extra else 0)
         runs.append((at * 128, size * 128))
         at += size
     return runs
@@ -259,6 +259,10 @@
     for target in targets:
         pl.semaphore_signal(barrier, inc=1, device_id=target, device_id_type=MESH)
     pl.semaphore_wait(barrier, len(targets))
+
+
+LONGER = (0, 2, 2, 1)
+TURNED = {(2, 0), (2, 2), (3, 1)}
 
 
 class Gather:
@@ -269,7 +273,8 @@
         self.sibling = device(1 - self.core, self.spot)
         self.near = neighbours(self.core, self.spot)
         self.jobs = [
-            [(i, part, cols) for part, cols in enumerate(cut(width // 128, 3))] for i, width in enumerate(widths)
+            [(i, part, cols) for part, cols in enumerate(cut(width // 128, 3, LONGER[i]))]
+            for i, width in enumerate(widths)
         ]
         self.forwards = [[] for _ in widths]
 
@@ -297,11 +302,15 @@
             axis = (part + phase) % 3
             done = [(part + p) % 3 for p in range(phase)]
             sides = [self.near[axis, by] for by in (1, 3, 2)]
-            halves_of = [(cols[0] + at, size) for at, size in cut(cols[1] // 128, 2)]
+            halves_of = [(cols[0] + at, size) for at, size in cut(cols[1] // 128, 2, (i, part) in TURNED)]
             yield i, part, cols, done, sides, halves_of
 
     def begin(self, item, phase):
-        for i, part, cols, done, (right, left, _), two in self.plan(item, phase):
+        for i, part, cols, done, (right, left, far), two in self.plan(item, phase):
+            if phase == 0:
+                for side, there in (("f", far), ("r", right), ("l", left)):
+                    self.push((i, part, phase, side), there[1], i, done, self.spot, cols)
+                continue
             for step, (a, b) in enumerate(((0, 1), (1, 0))):
                 self.push((i, part, phase, "r", step), right[1], i, done, self.spot, two[a])
                 self.push((i, part, phase, "l", step), left[1], i, done, self.spot, two[b])
@@ -319,6 +328,10 @@
 
     def finish(self, item, phase):
         for i, part, cols, done, (right, left, far), two in self.plan(item, phase):
+            if phase == 0:
+                for side, source in (("r", left), ("l", right), ("f", far)):
+                    self.sends.arrived((i, part, phase, side), self.block(i, done, source[0], cols), source[1])
+                continue
             for side, step, at, cc, source in (
                 ("r", 1, left, two[1], left),
                 ("l", 1, right, two[0], right),
@@ -416,14 +429,14 @@
 
 
 def forward_kernel(
-    split_ref, got_ref, gain1_ref, gain2_ref, mask_ref, place_ref, pers_ref,
+    split_ref, sent_ref, gain1_ref, gain2_ref, mask_ref, place_ref, pers_ref,
     mine0, mine1, mine2, mine3,
     g0_ref, g1_ref, g2_ref, g3_ref, proj_ref, x_ref, h1_ref, lat_ref, wf_ref, lw_ref, back_ref, dz_ref, dmid_ref,
     grads_ref,
-    flat, d_ref, dec_ref, dect_ref, inc0, inc1, inc2, inc3, stage0, stage1, stage2, stage3,
+    got, flat, d_ref, dec_ref, dect_ref, inc0, inc1, inc2, inc3, stage0, stage1, stage2, stage3,
     w_buf, up_buf, down_buf, z_ref, wup_buf, wd_buf, lead_buf,
     x2_ref, h2_ref, inv_ref, lat_out_ref, lat_up_ref, dl_down_ref, acc_ref, lat_acc_ref, dh_ref, dlat_ref,
-    send_sem, recv_sem, local_sem, w_sem, j_sem,
+    send_sem, recv_sem, local_sem, w_sem, j_sem, token_send, token_recv,
 ):
     step = pl.program_id(0)
     mine, inc = (mine0, mine1, mine2, mine3), (inc0, inc1, inc2, inc3)
@@ -433,6 +446,14 @@
     core, spot = ring.core, ring.spot
     other = 1 - core
     items = range(4)
+    me = lax.axis_index("fsdp")
+
+    def token_copy(k):
+        target = (me + k) % N_DEV
+        return pltpu.make_async_remote_copy(
+            src_ref=sent_ref.at[target], dst_ref=got.at[me], send_sem=token_send.at[k], recv_sem=token_recv.at[k],
+            device_id=(target,), device_id_type=MESH,
+        )
 
     def head_loads(h, slot):
         half, place = h // 4, pl.multiple_of((h % 4) * HCOLS, 128)
@@ -469,7 +490,14 @@
 
     @pl.when(step == 0)
     def _():
-        greet([ring.sibling] + [there[1] for there in ring.near.values()])
+        barrier = pltpu.get_barrier_semaphore()
+
+        def signal(k, carry):
+            pl.semaphore_signal(barrier, inc=1, device_id=((me + k) % N_DEV,), device_id_type=MESH)
+            return carry
+
+        lax.fori_loop(1, N_DEV, signal, 0)
+        pl.semaphore_wait(barrier, N_DEV - 1)
         for i in items:
             sends.start(("pair", i), lambda i=i: (mine[i].at[other], inc[i], ring.sibling))
         own_copy = lambda i: pltpu.make_async_copy(
@@ -485,24 +513,32 @@
         for i in items:
             own_copy(i).wait()
             ring.begin(i, 0)
-        flat[...] = got_ref[...].astype(F32).reshape(N_DEV * TOKEN_ROWS, 128)
-
         def columns(first, count):
             return jnp.concatenate(
                 [flat[pl.ds(first + c, N_DEV, stride=TOKEN_ROWS), :].astype(BF) for c in range(count)], axis=1
             )
 
-        for i in items:
-            ring.relay(i, 0)
-        for i in items:
+        ring.finish(0, 0)
+        ring.begin(0, 1)
+
+        def send_tokens(k, carry):
+            token_copy(k).start()
+            return carry
+
+        def take_tokens(k, carry):
+            token_copy(k).wait()
+            return carry
+
+        lax.fori_loop(1, N_DEV, send_tokens, 0)
+        got[me] = sent_ref[me]
+        for i in items[1:]:
             ring.finish(i, 0)
-            ring.begin(i, 1)
-        for i in items:
-            ring.relay(i, 1)
+        ring.relay(0, 1)
         ring.finish(0, 1)
         ring.begin(0, 2)
-        for i in items[1:]:
-            ring.finish(i, 1)
+        ring.begin(1, 1)
+        lax.fori_loop(1, N_DEV, take_tokens, 0)
+        flat[...] = got[...].astype(F32).reshape(N_DEV * TOKEN_ROWS, 128)
         rates = columns(4 * D // 128, 1)
         for m in range(MB):
             s = slice(m * GROUP, (m + 1) * GROUP)
@@ -515,8 +551,12 @@
         normed, _ = norm_fwd(x_ref[...].astype(F32), gain1_ref[...])
         h1_ref[...] = normed.astype(BF)
         ring.relay(0, 2)
+        ring.relay(1, 1)
+        for i in items[2:]:
+            ring.begin(i, 1)
+        ring.finish(0, 2)
+        ring.finish(1, 1)
         ring.begin(1, 2)
-        ring.finish(0, 2)
         ring.received(0)
         for copy in head_loads(0, 0):
             copy.start()
@@ -528,19 +568,20 @@
             s = slice(part * AR, (part + 1) * AR)
             lat_ref[:, s] = (latent[:, s] * mask).astype(BF)
 
+    @pl.when(step == 1)
+    def _():
+        for i in items[2:]:
+            ring.relay(i, 1)
+
     @pl.when(step == 3)
     def _():
         ring.relay(1, 2)
+
+    @pl.when(step == 6)
+    def _():
+        ring.finish(2, 1)
         ring.begin(2, 2)
-
-    @pl.when(step == FSTEPS - 1)
-    def _():
-        ring.finish(1, 2)
-        ring.received(1)
-        for copy in (lead_load(), up_load(0), wall_load(0)):
-            copy.start()
-        ring.relay(2, 2)
-        ring.begin(3, 2)
+        ring.finish(3, 1)
 
     @pl.when(step < FSTEPS)
     def _():
@@ -584,7 +625,13 @@
 
     @pl.when(step == FSTEPS)
     def _():
+        ring.finish(1, 2)
+        ring.received(1)
+        for copy in (lead_load(), up_load(0), wall_load(0)):
+            copy.start()
         lead_load().wait()
+        ring.relay(2, 2)
+        ring.begin(3, 2)
         mask = mask_ref[...]
         z = z_ref[...]
         lat_out_ref[...] = (dot(z, out_down()) * mask).astype(BF)
@@ -685,11 +732,11 @@
         sends.drain()
 
 
-def forward_call(split, got, gain1, gain2, mask, place, persistent, mine):
+def forward_call(split, sent, gain1, gain2, mask, place, persistent, mine):
     once = pl.Buffered(1)
     whole = lambda *shape: pl.BlockSpec(shape, lambda s: (0,) * len(shape), pipeline_mode=once)
     hbm = pl.BlockSpec(memory_space=pl.ANY)
-    slots = 4 * (1 + 3 * (3 * 6 + 7))
+    slots = 4 * (1 + 3 * (3 + 2 * 6 + 7))
     return pl.pallas_call(
         forward_kernel,
         grid=(FSTEPS + BLOCKS,),
@@ -730,6 +777,7 @@
             whole(2, 64, 16, 896),
         ),
         scratch_shapes=[
+            pltpu.VMEM((N_DEV, TOKEN_ROWS, 128), BF),
             pltpu.VMEM((N_DEV * TOKEN_ROWS, 128), F32),
             pltpu.VMEM((ROWS, D), BF),
             pltpu.VMEM((ROWS, 3 * H), F32),
@@ -760,12 +808,14 @@
             pltpu.SemaphoreType.DMA((4,)),
             pltpu.SemaphoreType.DMA((2, 2)),
             pltpu.SemaphoreType.DMA((2, 2)),
+            pltpu.SemaphoreType.DMA((N_DEV,)),
+            pltpu.SemaphoreType.DMA((N_DEV,)),
         ],
         compiler_params=pltpu.CompilerParams(
             collective_id=0, has_side_effects=True, vmem_limit_bytes=VMEM_LIMIT
         ),
         name="gather_forward",
-    )(split, got, gain1, gain2, mask, place, persistent, *mine)
+    )(split, sent, gain1, gain2, mask, place, persistent, *mine)
 
 
 class Scatter:
@@ -856,7 +906,7 @@
     split_ref, x_ref, gain_ref, mask_ref, place_ref, proj_ref, dz_ref, dmid_ref, h1_ref, lat_ref,
     w_ref, down_ref, up_ref, pers_ref, wf_ref, lw_ref, ffn_ref, back_ref,
     act_out, grad_out, ffn_out, heads_out,
-    dh_ref, dlat_ref, dlat_half, dy_ref, grads_ref, *rest,
+    dh_ref, dlat_ref, dlat_half, grads_ref, *rest,
 ):
     step = pl.program_id(0)
     send_sem, recv_sem = rest[-2:]
@@ -896,7 +946,7 @@
         d_mk = unit_bwd(d_kn, pieces[3], k_inv)
         d_mq = unit_bwd(d_qn, pieces[5], q_inv)
         dy = [item.astype(BF) for item in (d_q, d_k, d_v, d_mk, d_mv, d_mq, d_open)]
-        dy_ref[step] = jnp.concatenate(dy, axis=1)
+        dh_ref[...] += dot(jnp.concatenate(dy, axis=1), w_ref[0], NT)
         first = pl.multiple_of(step * 8, 8)
         for part in range(7):
             s = slice(part * AR, (part + 1) * AR)
@@ -911,6 +961,7 @@
         ex_act.fill(0, flat, [back_ref[...]])
         ex_act.launch(0)
         first_sums.pair()
+        dh_ref[...] = jnp.zeros_like(dh_ref)
         dlat_ref[...] = jnp.zeros_like(dlat_ref)
 
     @pl.when(step == 1)
@@ -947,11 +998,9 @@
         ex_act.land(3)
         act_out[...] = ex_act.bufs[4][...]
 
-    @pl.when(step < H)
-    def _():
-        one_head()
-
-    @pl.when(step == H)
+    one_head()
+
+    @pl.when(step == H - 1)
     def _():
         mask = mask_ref[...]
         for p in range(7):
@@ -959,42 +1008,32 @@
             dlat_half[:, s] = (dlat_ref[:, s] * mask).astype(BF)
         grads_ref[0] = dot(h1_ref[...], dlat_half[...], TN).reshape(64, 16, 7 * AR).astype(BF)
         last_sums.pair()
-        dh_ref[...] = dot(dlat_half[...], down_ref[0], NT)
-
-    @pl.when(step == H + 2)
-    def _():
-        last_sums.add_pair()
-        last_sums.send(1)
-
-    @pl.when(step >= H)
-    def _():
-        dh_ref[...] += dot(dy_ref[step - H], w_ref[0], NT)
-
-    @pl.when(step == 2 * H - 1)
-    def _():
+        dh = dh_ref[...] + dot(dlat_half[...], down_ref[0], NT)
         x = x_ref[...].astype(F32)
         inv = lax.rsqrt(jnp.mean(x * x, axis=-1, keepdims=True) + EPS)
-        dx = (dmid_ref[...] + norm_bwd(dh_ref[...], x, inv, gain_ref[...])).astype(BF)
+        dx = (dmid_ref[...] + norm_bwd(dh, x, inv, gain_ref[...])).astype(BF)
         ex_grad.fill(
             0, flat, [dot(place_ref[m], dx[m * GROUP : (m + 1) * GROUP]) for m in range(MB)]
         )
         ex_grad.launch(0)
+        last_sums.add_pair()
+        ex_grad.land(0)
+        ex_grad.launch(1)
+        last_sums.send(1)
         first_sums.swapped()
         ffn_out[...] = first_sums.out[...]
-        ex_grad.land(0)
-        ex_grad.launch(1)
+        ex_grad.land(1)
+        ex_grad.launch(2)
         last_sums.add(1)
         last_sums.send(2)
-        ex_grad.land(1)
-        ex_grad.launch(2)
+        ex_grad.land(2)
+        ex_grad.launch(3)
         last_sums.add(2)
         last_sums.send(3)
-        ex_grad.land(2)
-        ex_grad.launch(3)
+        ex_grad.land(3)
+        grad_out[...] = ex_grad.bufs[4][...]
         last_sums.add(3)
         last_sums.swap()
-        ex_grad.land(3)
-        grad_out[...] = ex_grad.bufs[4][...]
         last_sums.swapped()
         heads_out[...] = last_sums.out[...]
         sends.drain()
@@ -1003,8 +1042,7 @@
 def backward_call(split, x, gain, mask, place, proj, dz, dmid, h1, lat, a1, persistent, wf, lw, grads_ffn, back):
     once = pl.Buffered(1)
     whole = lambda *shape: pl.BlockSpec(shape, lambda s: (0,) * len(shape), pipeline_mode=once)
-    head = lambda s: jnp.minimum(s, H - 1)
-    late = lambda s: jnp.maximum(s - H, 0)
+    head = lambda s: s
     buffers = [
         pltpu.VMEM((2, 16, 896), F32),
         pltpu.VMEM((4, 16, 16, 896), BF),
@@ -1018,7 +1056,7 @@
     slots = 2 * (4 + 3 * 9 + 1) + 2 * (1 + 3 * 6)
     return pl.pallas_call(
         backward_kernel,
-        grid=(2 * H,),
+        grid=(H,),
         out_shape=(
             jax.ShapeDtypeStruct((4, 4, 4, 16, 256), BF),
             jax.ShapeDtypeStruct((4, 4, 4, 16, 256), BF),
@@ -1036,7 +1074,7 @@
             whole(ROWS, D),
             whole(ROWS, D),
             whole(ROWS, 7 * AR),
-            pl.BlockSpec((1, D, HCOLS), lambda s: (late(s) // 4, 0, late(s) % 4)),
+            pl.BlockSpec((1, D, HCOLS), lambda s: (s // 4, 0, s % 4)),
             pl.BlockSpec((1, D, HCOLS), lambda s: (0, 0, 4), pipeline_mode=once),
             pl.BlockSpec((1, HEAD, HCOLS), lambda s: (1, head(s), 4)),
             pl.BlockSpec((2, NP, HEAD), lambda s: (0, 0, head(s))),
@@ -1055,7 +1093,6 @@
             pltpu.VMEM((ROWS, D), F32),
             pltpu.VMEM((ROWS, 7 * AR), F32),
             pltpu.VMEM((ROWS, 7 * AR), BF),
-            pltpu.VMEM((H, ROWS, HCOLS), BF),
             pltpu.VMEM((2, 64, 16, 896), BF),
         ]
         + buffers * 2
@@ -1082,17 +1119,10 @@
 def pack_kernel(
     lengths_ref, ids_ref, route_ref, tok_ref, cot_ref, decays_ref,
     w_in, w_out, w_up, w_down, in_down, in_up, out_down, out_up, up_down, up_up, down_down, down_up,
-    got_ref, item0, item1, item2, item3, to_ref, place_ref, mask_ref, split_ref,
-    flat, wide, sent, send_sem, recv_sem, own_sem,
+    sent, item0, item1, item2, item3, to_ref, place_ref, mask_ref, split_ref,
+    flat, wide,
 ):
     me = lax.axis_index("fsdp")
-    barrier = pltpu.get_barrier_semaphore()
-
-    def signal(k, carry):
-        pl.semaphore_signal(barrier, inc=1, device_id=((me + k) % N_DEV,), device_id_type=MESH)
-        return carry
-
-    lax.fori_loop(1, N_DEV, signal, 0)
 
     below = lax.broadcasted_iota(jnp.int32, (GROUP, GROUP), 0)
     along = lax.broadcasted_iota(jnp.int32, (GROUP, GROUP), 1)
@@ -1110,25 +1140,6 @@
         flat[pl.ds(j, N_DEV, stride=TOKEN_ROWS), :] = jnp.zeros((N_DEV, 128), F32)
     sent[...] = flat[...].reshape(N_DEV, TOKEN_ROWS, 128).astype(BF)
 
-    def copy(k):
-        target = (me + k) % N_DEV
-        return pltpu.make_async_remote_copy(
-            src_ref=sent.at[target], dst_ref=got_ref.at[me], send_sem=send_sem.at[k], recv_sem=recv_sem.at[k],
-            device_id=(target,), device_id_type=MESH,
-        )
-
-    def begin(k, carry):
-        copy(k).start()
-        return carry
-
-    def end(k, carry):
-        copy(k).wait()
-        return carry
-
-    pl.semaphore_wait(barrier, N_DEV - 1)
-    lax.fori_loop(1, N_DEV, begin, 0)
-    own = pltpu.make_async_copy(sent.at[me], got_ref.at[me], own_sem)
-    own.start()
     for m in range(MB):
         blocks = route_ref[m]
         landing = jnp.sum(jnp.where(blocks // GROUP == me, blocks % GROUP, 0), axis=1, keepdims=True)
@@ -1206,9 +1217,6 @@
         items[k][1, :, at + 512 : at + 640] = dd[s]
         items[k][1, :, at + 640 : at + 768] = jnp.zeros((8, 128), F32)
 
-    own.wait()
-    lax.fori_loop(1, N_DEV, end, 0)
-
 
 def pack_call(lengths, ids, route, tokens, cotangent, decays, weights):
     smem, vmem = pl.BlockSpec(memory_space=pltpu.SMEM), pl.BlockSpec(memory_space=pltpu.VMEM)
@@ -1223,18 +1231,12 @@
             jax.ShapeDtypeStruct((MB,), F32),
         ),
         in_specs=[smem] * 2 + [vmem] * (4 + len(weights)),
-        out_specs=(pl.BlockSpec(memory_space=pl.ANY),) + (vmem,) * 7 + (smem,),
+        out_specs=(vmem,) * 8 + (smem,),
         scratch_shapes=[
             pltpu.VMEM((N_DEV * TOKEN_ROWS, 128), F32),
             pltpu.VMEM((8, 2 * FF), F32),
-            pltpu.VMEM((N_DEV, TOKEN_ROWS, 128), BF),
-            pltpu.SemaphoreType.DMA((N_DEV,)),
-            pltpu.SemaphoreType.DMA((N_DEV,)),
-            pltpu.SemaphoreType.DMA,
         ],
-        compiler_params=pltpu.CompilerParams(
-            collective_id=2, has_side_effects=True, vmem_limit_bytes=VMEM_LIMIT
-        ),
+        compiler_params=pltpu.CompilerParams(vmem_limit_bytes=VMEM_LIMIT),
         name="pack",
     )(lengths, ids, route, tokens, cotangent, decays, *weights)
 
@@ -1311,12 +1313,12 @@
     views = (None,) * 5 + (turned, None, turned, None, lambda value: value.transpose(2, 0, 1), turned, turned)
     back_views = views[:9] + (lambda value: value.transpose(1, 2, 0), turned, turned)
     viewed = [item if view is None else view(item) for item, view in zip(weights, views)]
-    got, *items, to, place, mask, split = pack_call(
+    sent, *items, to, place, mask, split = pack_call(
         lengths[:, 0], adapter_ids[:, 0], route.reshape(MB, N_DEV, GROUP), tokens, cotangent, turned(decays), viewed
     )
     gain_mix, gain_ffn = gain_mix[None, :], gain_ffn[None, :]
     a1, _, _, _, proj, x, h1, lat, wf, lw, back, dz, dmid, grads_ffn = forward_call(
-        split, got, gain_mix, gain_ffn, mask, place, persistent, items
+        split, sent, gain_mix, gain_ffn, mask, place, persistent, items
     )
     act, grad, ffn_sums, heads_sums = backward_call(
         split, x, gain_mix, mask, place, proj, dz, dmid, h1, lat, a1.reshape(2, D, WIDTHS[0]), persistent, wf, lw,

time: 248 us -> 237 us (0.956)
  Pallas kernels: 245 us -> 234 us
    pallas_call x1, Pallas kernels: 39.6 us -> 4.39 us  [pack_call(): pl.pallas_call(pack_kernel, out_shape=(jax.ShapeDtypeStruct((N_DEV, TOKEN...]
    pallas_call x1, Pallas kernels: 134 us -> 158 us  [forward_call(): pl.pallas_call(forward_kernel, grid=(FSTEPS + BLOCKS,), out_shape=tuple((...]
where the time goes in v1:
time: 237 us
  Pallas kernels  234 us (99%)
    pallas_call x1, Pallas kernels, forward_call(): pl.pallas_call(forward_kernel, grid=(FSTEPS + BLOCKS,), out_shape=tuple((...  158 us
    pallas_call x1, Pallas kernels, backward_call(): pl.pallas_call(backward_kernel, grid=(H,), out_shape=(jax.ShapeDtypeStruc...  67.8 us

profile of v1, /device:TPU:1, one launch (start us, length us, event | category | flops | bytes accessed | tf_op | source)
XLA Modules:
  0.0 236.7 jit_solution(2780720600918938325)
XLA Ops:
  0.6 1.6 copy.33
  2.2 4.4 %pack.1 = (bf16[128,48,128]{2,1,0:T(8,128)(2,1)}, f32[2,8,4480]{2,1,0:T(8,128)}, f32[2,8,2816]{2,1,0:T(8,128)}, f32[2,8,1792]{2,1,0:T(8,128)}, f32[2,8,1792]{2,1...) custom-call(s32[2,2]{1,0:T(2,128)} %bitcast.35, ...), custom_call_target="tpu_custom_call" | custom-call | tf_op jit(solution)/shard_map/pack/pallas_call | solution.py:1223
  6.6 158.3 %gather_forward.1 = (bf16[2,4,4,4,16,4480]{5,4,3,2,1,0:T(8,128)(2,1)}, bf16[2,4,4,4,16,2816]{5,4,3,2,1,0:T(8,128)(2,1)}, bf16[2,4,4,4,16,1792]{5,4,3,2,1,0:T(8,1...) custom-call(f32[2]{0:T(128)} %get-tuple-element.45.split_ref, ...), custom_call_target="tpu_custom_call" | custom-call | tf_op jit(solution)/shard_map/gather_forward/pallas_call | solution.py:740
  164.9 67.8 %backward_scatter.1 = (bf16[4,4,4,16,256]{4,3,2,1,0:T(8,128)(2,1)}, bf16[4,4,4,16,256]{4,3,2,1,0:T(8,128)(2,1)}, f32[2,16,896]{2,1,0:T(8,128)}, f32[2,16,896]{2,1,0:T(8,128)}) custom-call(f32[2]{0:T(128)} %get-tuple-element.45.split_ref, bf16[256,1024]{1,0:T(8,128)(2,1)} %get-tuple-element.53.x_ref, f32[1,1024]{1,0:T(1,128)} %bitcast.32, ...), custom_call_target="tpu_custom_call" | custom-call | tf_op jit(solution)/shard_map/backward_scatter/pallas_call | solution.py:1057
  232.7 4.0 %unpack.1 = (bf16[2,128,1024]{2,1,0:T(8,128)(2,1)}, bf16[2,128,1024]{2,1,0:T(8,128)(2,1)}, f32[8,8,112]{2,1,0:T(8,128)}, f32[8,8,112]{2,1,0:T(8,128)}, f32[8,8,1...) custom-call(s32[1]{0:T(128)} %bitcast.core_ref, ...), custom_call_target="tpu_custom_call" | custom-call | tf_op jit(solution)/shard_map/unpack/pallas_call | solution.py:1292

commit v2 on v1

--- a/solution.py
+++ b/solution.py
@@ -421,19 +421,82 @@
 BY_CORE = [(0, 128, 0), (128, 128, 1)]
 
 
+class RowExchange:
+    RADIX = {"x": 4, "z": 4, "y": 4, "c": 2}
+    NATURAL = ("x", "z", "y", "c")
+
+    def __init__(self, sends, key, src, dst):
+        self.sends, self.key, self.src, self.dst = sends, key, src, dst
+        self.core, self.spot = position()
+        self.mine, self.theirs = pl.ds(2 * self.core, 2), pl.ds(2 * (1 - self.core), 2)
+        self.sibling = device(1 - self.core, self.spot)
+        self.near = neighbours(self.core, self.spot)
+
+    def order(self, stage):
+        lead = "c" if stage == 0 else AXES[stage - 1]
+        return (lead,) + tuple(name for name in self.NATURAL if name != lead)
+
+    def shuffle(self, new, old, rows):
+        rest = lax.broadcasted_iota(jnp.int32, (N_DEV, N_DEV), 0)
+        digit = {}
+        for name in reversed(new):
+            digit[name] = rest % self.RADIX[name]
+            rest = rest // self.RADIX[name]
+        index = 0
+        for name in old:
+            index = index * self.RADIX[name] + digit[name]
+        onehot = (index == lax.broadcasted_iota(jnp.int32, (N_DEV, N_DEV), 1)).astype(BF)
+        return dot(onehot, rows).astype(BF)
+
+    def launch(self, stage, value=None):
+        if stage == 0:
+            self.src[0] = self.shuffle(self.order(0), self.NATURAL, value).reshape(4, 32, 128)
+            self.sends.start(
+                (self.key, 0), lambda: (self.src.at[0, self.theirs], self.dst.at[0, self.mine], self.sibling)
+            )
+            return
+        rows = self.dst[stage - 1].reshape(N_DEV, 128)
+        self.src[stage] = self.shuffle(self.order(stage), self.order(stage - 1), rows).reshape(4, 32, 128)
+        axis = stage - 1
+        for by in (2, 1, 3):
+            there, target = self.near[axis, by]
+            self.sends.start(
+                (self.key, stage, by),
+                lambda there=there, target=target: (
+                    self.src.at[stage, there[axis]],
+                    self.dst.at[stage, self.spot[axis]],
+                    target,
+                ),
+            )
+
+    def land(self, stage):
+        if stage == 0:
+            self.dst[0, self.mine] = self.src[0, self.mine]
+            self.sends.arrived((self.key, 0), self.dst.at[0, self.theirs], self.sibling)
+            return
+        axis = stage - 1
+        self.dst[stage, self.spot[axis]] = self.src[stage, self.spot[axis]]
+        for by in (2, 1, 3):
+            there, source = self.near[axis, 4 - by]
+            self.sends.arrived((self.key, stage, by), self.dst.at[stage, there[axis]], source)
+
+    def rows(self):
+        return self.shuffle(self.NATURAL, self.order(3), self.dst[3].reshape(N_DEV, 128))
+
+
 WALL = 768
-TOKEN_ROWS = 48
+TOKEN_ROWS = 32
 WIDTHS = (4 * HCOLS + 7 * AR, D + FB + WALL, FB + WALL, FB + WALL)
 FSTEPS = H
 BLOCKS = FFP // FB
 
 
 def forward_kernel(
-    split_ref, sent_ref, gain1_ref, gain2_ref, mask_ref, place_ref, pers_ref,
+    split_ref, sent_ref, rates_ref, gain1_ref, gain2_ref, mask_ref, place_ref, pers_ref,
     mine0, mine1, mine2, mine3,
     g0_ref, g1_ref, g2_ref, g3_ref, proj_ref, x_ref, h1_ref, lat_ref, wf_ref, lw_ref, back_ref, dz_ref, dmid_ref,
     grads_ref,
-    got, flat, d_ref, dec_ref, dect_ref, inc0, inc1, inc2, inc3, stage0, stage1, stage2, stage3,
+    rate_src, rate_dst, got, flat, d_ref, dec_ref, dect_ref, inc0, inc1, inc2, inc3, stage0, stage1, stage2, stage3,
     w_buf, up_buf, down_buf, z_ref, wup_buf, wd_buf, lead_buf,
     x2_ref, h2_ref, inv_ref, lat_out_ref, lat_up_ref, dl_down_ref, acc_ref, lat_acc_ref, dh_ref, dlat_ref,
     send_sem, recv_sem, local_sem, w_sem, j_sem, token_send, token_recv,
@@ -447,6 +510,7 @@
     other = 1 - core
     items = range(4)
     me = lax.axis_index("fsdp")
+    decay_rows = RowExchange(sends, "rates", rate_src, rate_dst)
 
     def token_copy(k):
         target = (me + k) % N_DEV
@@ -510,36 +574,45 @@
             last = jnp.where(core == 0, theirs, own)
             stage[i][...] = jnp.concatenate([first, last], axis=0).astype(BF)
             own_copy(i).start()
-        for i in items:
-            own_copy(i).wait()
-            ring.begin(i, 0)
+        def send_tokens(k, carry):
+            token_copy(k).start()
+            return carry
+
+        def take_tokens(k, carry):
+            token_copy(k).wait()
+            return carry
+
         def columns(first, count):
             return jnp.concatenate(
                 [flat[pl.ds(first + c, N_DEV, stride=TOKEN_ROWS), :].astype(BF) for c in range(count)], axis=1
             )
 
+        for i in items:
+            own_copy(i).wait()
+            ring.begin(i, 0)
+        decay_rows.launch(0, rates_ref[...])
+        lax.fori_loop(1, 43, send_tokens, 0)
         ring.finish(0, 0)
         ring.begin(0, 1)
-
-        def send_tokens(k, carry):
-            token_copy(k).start()
-            return carry
-
-        def take_tokens(k, carry):
-            token_copy(k).wait()
-            return carry
-
-        lax.fori_loop(1, N_DEV, send_tokens, 0)
-        got[me] = sent_ref[me]
+        decay_rows.land(0)
+        decay_rows.launch(1)
+        lax.fori_loop(43, 85, send_tokens, 0)
         for i in items[1:]:
             ring.finish(i, 0)
         ring.relay(0, 1)
+        decay_rows.land(1)
+        decay_rows.launch(2)
+        lax.fori_loop(85, N_DEV, send_tokens, 0)
+        got[me] = sent_ref[me]
         ring.finish(0, 1)
+        decay_rows.land(2)
+        decay_rows.launch(3)
         ring.begin(0, 2)
         ring.begin(1, 1)
         lax.fori_loop(1, N_DEV, take_tokens, 0)
         flat[...] = got[...].astype(F32).reshape(N_DEV * TOKEN_ROWS, 128)
-        rates = columns(4 * D // 128, 1)
+        decay_rows.land(3)
+        rates = decay_rows.rows()
         for m in range(MB):
             s = slice(m * GROUP, (m + 1) * GROUP)
             x_ref[s, :] = dot(place_ref[m], columns(m * D // 128, D // 128), TN).astype(BF)
@@ -732,11 +805,11 @@
         sends.drain()
 
 
-def forward_call(split, sent, gain1, gain2, mask, place, persistent, mine):
+def forward_call(split, sent, rates, gain1, gain2, mask, place, persistent, mine):
     once = pl.Buffered(1)
     whole = lambda *shape: pl.BlockSpec(shape, lambda s: (0,) * len(shape), pipeline_mode=once)
     hbm = pl.BlockSpec(memory_space=pl.ANY)
-    slots = 4 * (1 + 3 * (3 + 2 * 6 + 7))
+    slots = 4 * (1 + 3 * (3 + 2 * 6 + 7)) + 1 + 3 * 3
     return pl.pallas_call(
         forward_kernel,
         grid=(FSTEPS + BLOCKS,),
@@ -756,6 +829,7 @@
         in_specs=[
             pl.BlockSpec(memory_space=pltpu.SMEM),
             whole(N_DEV, TOKEN_ROWS, 128),
+            whole(N_DEV, 128),
             whole(1, D),
             whole(1, D),
             whole(ROWS, AR),
@@ -777,6 +851,8 @@
             whole(2, 64, 16, 896),
         ),
         scratch_shapes=[
+            pltpu.VMEM((4, 4, 32, 128), BF),
+            pltpu.VMEM((4, 4, 32, 128), BF),
             pltpu.VMEM((N_DEV, TOKEN_ROWS, 128), BF),
             pltpu.VMEM((N_DEV * TOKEN_ROWS, 128), F32),
             pltpu.VMEM((ROWS, D), BF),
@@ -815,7 +891,7 @@
             collective_id=0, has_side_effects=True, vmem_limit_bytes=VMEM_LIMIT
         ),
         name="gather_forward",
-    )(split, sent, gain1, gain2, mask, place, persistent, *mine)
+    )(split, sent, rates, gain1, gain2, mask, place, persistent, *mine)
 
 
 class Scatter:
@@ -1119,7 +1195,7 @@
 def pack_kernel(
     lengths_ref, ids_ref, route_ref, tok_ref, cot_ref, decays_ref,
     w_in, w_out, w_up, w_down, in_down, in_up, out_down, out_up, up_down, up_up, down_down, down_up,
-    sent, item0, item1, item2, item3, to_ref, place_ref, mask_ref, split_ref,
+    sent, rates_out, item0, item1, item2, item3, to_ref, place_ref, mask_ref, split_ref,
     flat, wide,
 ):
     me = lax.axis_index("fsdp")
@@ -1135,9 +1211,7 @@
                 flat[pl.ds(first + j, N_DEV, stride=TOKEN_ROWS), :] = value[:, j * 128 : (j + 1) * 128]
     rates = [dot(to_ref[m], decays_ref[m], NT) for m in range(MB)]
     rates = jnp.concatenate(rates + [jnp.zeros((GROUP, 128 - MB * 3 * H), F32)], axis=1)
-    flat[pl.ds(4 * D // 128, N_DEV, stride=TOKEN_ROWS), :] = rates
-    for j in range(4 * D // 128 + 1, TOKEN_ROWS):
-        flat[pl.ds(j, N_DEV, stride=TOKEN_ROWS), :] = jnp.zeros((N_DEV, 128), F32)
+    rates_out[...] = rates.astype(BF)
     sent[...] = flat[...].reshape(N_DEV, TOKEN_ROWS, 128).astype(BF)
 
     for m in range(MB):
@@ -1222,7 +1296,10 @@
     smem, vmem = pl.BlockSpec(memory_space=pltpu.SMEM), pl.BlockSpec(memory_space=pltpu.VMEM)
     return pl.pallas_call(
         pack_kernel,
-        out_shape=(jax.ShapeDtypeStruct((N_DEV, TOKEN_ROWS, 128), BF),)
+        out_shape=(
+            jax.ShapeDtypeStruct((N_DEV, TOKEN_ROWS, 128), BF),
+            jax.ShapeDtypeStruct((N_DEV, 128), BF),
+        )
         + tuple(jax.ShapeDtypeStruct((2, 8, width), F32) for width in WIDTHS)
         + (
             jax.ShapeDtypeStruct((MB, GROUP, GROUP), BF),
@@ -1231,7 +1308,7 @@
             jax.ShapeDtypeStruct((MB,), F32),
         ),
         in_specs=[smem] * 2 + [vmem] * (4 + len(weights)),
-        out_specs=(vmem,) * 8 + (smem,),
+        out_specs=(vmem,) * 9 + (smem,),
         scratch_shapes=[
             pltpu.VMEM((N_DEV * TOKEN_ROWS, 128), F32),
             pltpu.VMEM((8, 2 * FF), F32),
@@ -1313,12 +1390,12 @@
     views = (None,) * 5 + (turned, None, turned, None, lambda value: value.transpose(2, 0, 1), turned, turned)
     back_views = views[:9] + (lambda value: value.transpose(1, 2, 0), turned, turned)
     viewed = [item if view is None else view(item) for item, view in zip(weights, views)]
-    sent, *items, to, place, mask, split = pack_call(
+    sent, rates, *items, to, place, mask, split = pack_call(
         lengths[:, 0], adapter_ids[:, 0], route.reshape(MB, N_DEV, GROUP), tokens, cotangent, turned(decays), viewed
     )
     gain_mix, gain_ffn = gain_mix[None, :], gain_ffn[None, :]
     a1, _, _, _, proj, x, h1, lat, wf, lw, back, dz, dmid, grads_ffn = forward_call(
-        split, sent, gain_mix, gain_ffn, mask, place, persistent, items
+        split, sent, rates, gain_mix, gain_ffn, mask, place, persistent, items
     )
     act, grad, ffn_sums, heads_sums = backward_call(
         split, x, gain_mix, mask, place, proj, dz, dmid, h1, lat, a1.reshape(2, D, WIDTHS[0]), persistent, wf, lw,

time: 237 us -> 231 us (0.975)
  Pallas kernels: 234 us -> 229 us
    pallas_call x1, Pallas kernels: 158 us -> 151 us  [forward_call(): pl.pallas_call(forward_kernel, grid=(FSTEPS + BLOCKS,), out_shape=tuple((...]
where the time goes in v2:
time: 231 us
  Pallas kernels  229 us (99%)
    pallas_call x1, Pallas kernels, forward_call(): pl.pallas_call(forward_kernel, grid=(FSTEPS + BLOCKS,), out_shape=tuple((...  151 us
    pallas_call x1, Pallas kernels, backward_call(): pl.pallas_call(backward_kernel, grid=(H,), out_shape=(jax.ShapeDtypeStruc...  68.7 us

profile of v2, /device:TPU:1, one launch (start us, length us, event | category | flops | bytes accessed | tf_op | source)
XLA Modules:
  0.0 230.9 jit_solution(12071988069981685705)
XLA Ops:
  0.6 1.6 copy.33
  2.2 4.5 %pack.1 = (bf16[128,32,128]{2,1,0:T(8,128)(2,1)}, bf16[128,128]{1,0:T(8,128)(2,1)}, f32[2,8,4480]{2,1,0:T(8,128)}, f32[2,8,2816]{2,1,0:T(8,128)}, f32[2,8,1792]{...) custom-call(s32[2,2]{1,0:T(2,128)} %bitcast.35, ...), custom_call_target="tpu_custom_call" | custom-call | tf_op jit(solution)/shard_map/pack/pallas_call | solution.py:1297
  6.8 151.4 %gather_forward.1 = (bf16[2,4,4,4,16,4480]{5,4,3,2,1,0:T(8,128)(2,1)}, bf16[2,4,4,4,16,2816]{5,4,3,2,1,0:T(8,128)(2,1)}, bf16[2,4,4,4,16,1792]{5,4,3,2,1,0:T(8,1...) custom-call(f32[2]{0:T(128)} %get-tuple-element.46.split_ref, ...), custom_call_target="tpu_custom_call" | custom-call | tf_op jit(solution)/shard_map/gather_forward/pallas_call | solution.py:813
  158.2 68.7 %backward_scatter.1 = (bf16[4,4,4,16,256]{4,3,2,1,0:T(8,128)(2,1)}, bf16[4,4,4,16,256]{4,3,2,1,0:T(8,128)(2,1)}, f32[2,16,896]{2,1,0:T(8,128)}, f32[2,16,896]{2,1,0:T(8,128)}) custom-call(f32[2]{0:T(128)} %get-tuple-element.46.split_ref, bf16[256,1024]{1,0:T(8,128)(2,1)} %get-tuple-element.55.x_ref, f32[1,1024]{1,0:T(1,128)} %bitcast.32, ...), custom_call_target="tpu_custom_call" | custom-call | tf_op jit(solution)/shard_map/backward_scatter/pallas_call | solution.py:1133
  226.9 3.9 %unpack.1 = (bf16[2,128,1024]{2,1,0:T(8,128)(2,1)}, bf16[2,128,1024]{2,1,0:T(8,128)(2,1)}, f32[8,8,112]{2,1,0:T(8,128)}, f32[8,8,112]{2,1,0:T(8,128)}, f32[8,8,1...) custom-call(s32[1]{0:T(128)} %bitcast.core_ref, ...), custom_call_target="tpu_custom_call" | custom-call | tf_op jit(solution)/shard_map/unpack/pallas_call | solution.py:1369

commit v3 on v2

--- a/solution.py
+++ b/solution.py
@@ -904,16 +904,20 @@
         self.sibling = device(1 - self.core, self.spot)
         self.near = neighbours(self.core, self.spot)
         self.parts = [(part, pl.ds(*cols)) for part, cols in enumerate(cut(7, 3))]
+        self.slabs = [(by, self.slab(by)) for by in (2, 1, 3, 0)]
 
     def peers(self):
         return [self.sibling] + [there[1] for there in self.near.values()]
 
+    def slab(self, by):
+        return (self.spot[0] + by) % 4
+
     def pair(self):
-        for x in range(4):
+        for by, x in self.slabs:
             self.sends.start(
-                (self.key, "pair", x),
+                (self.key, "pair", by),
                 lambda x=x: (
-                    self.grads.at[self.other, pl.ds(16 * x, 16)],
+                    self.grads.at[self.other, pl.ds(pl.multiple_of(16 * x, 16), 16)],
                     self.inc0.at[x],
                     self.sibling,
                 ),
@@ -934,17 +938,23 @@
     def landing(self, phase, part, k):
         return (k,) + (slice(None),) * (4 - phase) + (self.parts[part][1],)
 
+    def send_one(self, phase, part, by):
+        axis = (part + phase - 1) % 3
+        to = self.near[axis, by]
+        k = (2, 1, 3).index(by)
+
+        def make():
+            ref, index = self.source(phase, part, to[0][axis])
+            return ref.at[index], self.inc[phase].at[self.landing(phase, part, k)], to[1]
+
+        self.sends.start((self.key, part, phase, by), make)
+
     def send(self, phase):
         for part, _ in self.parts:
-            axis = (part + phase - 1) % 3
-            for k, by in enumerate((2, 1, 3)):
-                to = self.near[axis, by]
-
-                def make(part=part, axis=axis, to=to, k=k):
-                    ref, index = self.source(phase, part, to[0][axis])
-                    return ref.at[index], self.inc[phase].at[self.landing(phase, part, k)], to[1]
-
-                self.sends.start((self.key, part, phase, by), make)
+            if phase == 1 and part == 0:
+                continue
+            for by in (2, 1, 3):
+                self.send_one(phase, part, by)
 
     def add(self, phase):
         for part, cs in self.parts:
@@ -964,10 +974,13 @@
                 self.out[self.core, :, cs] = acc
 
     def add_pair(self):
-        for x in range(4):
-            self.sends.arrived((self.key, "pair", x), self.inc0.at[x], self.sibling)
-            both = self.grads[self.core, pl.ds(16 * x, 16)].astype(F32) + self.inc0[x].astype(F32)
+        for by, x in self.slabs:
+            self.sends.arrived((self.key, "pair", by), self.inc0.at[x], self.sibling)
+            mine = self.grads[self.core, pl.ds(pl.multiple_of(16 * x, 16), 16)]
+            both = mine.astype(F32) + self.inc0[x].astype(F32)
             self.total[x] = both.reshape(4, 4, 16, 896).astype(BF)
+            if by:
+                self.send_one(1, 0, by)
 
     def swap(self):
         self.sends.start(

time: 231 us -> 234 us (1.013)
    pallas_call x1, Pallas kernels: 68.7 us -> 71.5 us  [backward_call(): pl.pallas_call(backward_kernel, grid=(H,), out_shape=(jax.ShapeDtypeStruc...]
where the time goes in v3:
time: 234 us
  Pallas kernels  231 us (99%)
    pallas_call x1, Pallas kernels, forward_call(): pl.pallas_call(forward_kernel, grid=(FSTEPS + BLOCKS,), out_shape=tuple((...  151 us
    pallas_call x1, Pallas kernels, backward_call(): pl.pallas_call(backward_kernel, grid=(H,), out_shape=(jax.ShapeDtypeStruc...  71.5 us

profile of v3, /device:TPU:1, one launch (start us, length us, event | category | flops | bytes accessed | tf_op | source)
XLA Modules:
  0.0 233.6 jit_solution(15741025822488675216)
XLA Ops:
  0.6 1.6 copy.33
  2.2 4.5 %pack.1 = (bf16[128,32,128]{2,1,0:T(8,128)(2,1)}, bf16[128,128]{1,0:T(8,128)(2,1)}, f32[2,8,4480]{2,1,0:T(8,128)}, f32[2,8,2816]{2,1,0:T(8,128)}, f32[2,8,1792]{...) custom-call(s32[2,2]{1,0:T(2,128)} %bitcast.35, ...), custom_call_target="tpu_custom_call" | custom-call | tf_op jit(solution)/shard_map/pack/pallas_call | solution.py:1310
  6.8 151.4 %gather_forward.1 = (bf16[2,4,4,4,16,4480]{5,4,3,2,1,0:T(8,128)(2,1)}, bf16[2,4,4,4,16,2816]{5,4,3,2,1,0:T(8,128)(2,1)}, bf16[2,4,4,4,16,1792]{5,4,3,2,1,0:T(8,1...) custom-call(f32[2]{0:T(128)} %get-tuple-element.46.split_ref, ...), custom_call_target="tpu_custom_call" | custom-call | tf_op jit(solution)/shard_map/gather_forward/pallas_call | solution.py:813
  158.2 71.5 %backward_scatter.1 = (bf16[4,4,4,16,256]{4,3,2,1,0:T(8,128)(2,1)}, bf16[4,4,4,16,256]{4,3,2,1,0:T(8,128)(2,1)}, f32[2,16,896]{2,1,0:T(8,128)}, f32[2,16,896]{2,1,0:T(8,128)}) custom-call(f32[2]{0:T(128)} %get-tuple-element.46.split_ref, bf16[256,1024]{1,0:T(8,128)(2,1)} %get-tuple-element.55.x_ref, f32[1,1024]{1,0:T(1,128)} %bitcast.32, ...), custom_call_target="tpu_custom_call" | custom-call | tf_op jit(solution)/shard_map/backward_scatter/pallas_call | solution.py:1146
  229.7 3.9 %unpack.1 = (bf16[2,128,1024]{2,1,0:T(8,128)(2,1)}, bf16[2,128,1024]{2,1,0:T(8,128)(2,1)}, f32[8,8,112]{2,1,0:T(8,128)}, f32[8,8,112]{2,1,0:T(8,128)}, f32[8,8,1...) custom-call(s32[1]{0:T(128)} %bitcast.core_ref, ...), custom_call_target="tpu_custom_call" | custom-call | tf_op jit(solution)/shard_map/unpack/pallas_call | solution.py:1382
